TPU v7x, 32 devices: a whole 2x2x4 slice. The times are simulated.
32 devices in a mesh: runs: 2 (over y), patch: 4 (over x, core), col: 4 (over z).
Axes of the slice: x: 2, y: 2, z: 4, core: 2. Of those that a mesh axis runs over, the one named last changes fastest.
Arguments:
- velocity: float32 [512, 3, 8192], P('runs', None, 'patch'), parts along dimension 0, may hold values from -6 to 6
- state: float32 [512, 8192], P(('runs', 'col'), 'patch'), parts along dimension 0, may hold values from 0.5 to 2
- friction: float32 [6, 8192], P('runs', 'patch'), parts along dimension 0, may hold values from 0.5 to 2
- near_src: int32 [64, 8], P('patch', 'col'), may hold values from 0 to 63, as said below
- near_block: bfloat16 [64, 8, 384, 384], P('patch', 'col'), may hold values from -0.109375 to 0.109375
- far_dest: int32 [4, 64, 4], P('col', 'patch'), may hold values from 0 to 127, as said below
- far_rank: int32 [4, 64, 4], P('col', 'patch'), may hold values from 1 to 32
- far_basis_v: bfloat16 [4, 64, 4, 32, 384], P('col', 'patch'), may hold values from -0.3125 to 0.3125
- far_target: int32 [4, 4, 4, 32], P('col', 'patch'), may hold values from -1 to 15, as said below
- far_basis_u: bfloat16 [4, 4, 4, 32, 32, 384], P('col', 'patch'), may hold values from -0.25 to 0.25
Outputs:
- velocity_rate: float32 [512, 3, 8192], P(('runs', 'col'), None, 'patch'), parts along dimension 0
There are 2 independent parts, one for each index of `runs`. A program takes and returns all parts, laid end to end along the dimension named above; an argument that names none is the same for every part. Nothing has to cross between parts.
Inputs may be any that keep to these rules, and one draw needn't show every extreme that they name: `near_src`: entry 0 of each row is the target cluster itself; every entry lies within 16 clusters of its target cluster; the last entry lies exactly 16 clusters away. `far_dest`: for one c and the source clusters of one index of patch the slot numbers are distinct, and one target row p gets all 32 numbers p * 32 to p * 32 + 31. far_target[c, p, q, s] is the local index within target row p of the target cluster of the far block of list c from source row q with slot number p * 32 + s, and -1 where no block has that slot.
All inputs are finite; a program needn't handle non-finite values.
Results may differ from a plain program's by a relative error of at most 0.0026.
Values may be sent and summed in bfloat16 or wider, within the bound.
A program may use at most 192 MiB of HBM per device.

v0:
```python
import jax
import jax.numpy as jnp
from jax import lax
from jax.sharding import PartitionSpec as P

CS = 128


damping = 0.5
speed_floor = 0.25


def padded(cells, sides, width):
    for axis, dim in sides:
        count = lax.axis_size(axis)
        ends = count - 1
        head = lax.slice_in_dim(cells, 0, width, axis=dim)
        tail = lax.slice_in_dim(cells, cells.shape[dim] - width, cells.shape[dim], axis=dim)
        cells = jnp.concatenate(
            [
                lax.ppermute(tail, axis, [(i, (i + 1) % count) for i in range(ends)]),
                cells,
                lax.ppermute(head, axis, [((i + 1) % count, i) for i in range(ends)]),
            ],
            axis=dim,
        )
    return cells


def shards(
    velocity,
    state,
    friction,
    near_src,
    near_block,
    far_dest,
    far_rank,
    far_basis_v,
    far_target,
    far_basis_u,
):
    members = velocity.shape[0]
    row_cells = velocity.shape[2]
    clusters = row_cells // CS
    near_count = near_src.shape[1]
    far_count = far_dest.shape[2]
    rank_width = far_basis_v.shape[3]
    patches = lax.axis_size("patch")
    capacity = far_target.shape[3]
    slot_total = patches * capacity
    member_share = state.shape[0]
    rounded = velocity.astype(jnp.bfloat16)
    extended = padded(rounded, (("patch", 2),), row_cells)
    extended = extended.reshape(members, 3, 3 * clusters, CS)
    first_cluster = lax.axis_index("patch") * clusters - clusters
    local_index = (near_src - first_cluster).reshape(-1)
    gathered = jnp.take(extended, local_index, axis=2).reshape(members, 3, clusters, near_count, CS)
    blocks = near_block.reshape(clusters, near_count, 3, CS, 3, CS)
    near_stress = jnp.einsum(
        "mctje,tjadce->matd", gathered, blocks, preferred_element_type=jnp.float32
    )
    own_view = rounded.reshape(members, 3, clusters, CS)
    basis_v = far_basis_v.reshape(clusters, far_count, rank_width, 3, CS)
    coeffs = jnp.einsum("tjkce,mcte->tjkm", basis_v, own_view, preferred_element_type=jnp.float32)
    live_rank = (
        jnp.arange(rank_width, dtype=jnp.int32)[None, None, :]
        < far_rank.reshape(clusters, far_count)[:, :, None]
    )
    coeffs = jnp.where(live_rank[..., None], coeffs, 0.0).astype(jnp.bfloat16)
    outgoing = jnp.zeros((slot_total, rank_width, members), jnp.bfloat16)
    outgoing = outgoing.at[far_dest.reshape(-1)].set(
        coeffs.reshape(clusters * far_count, rank_width, members)
    )
    arrived = lax.all_to_all(
        outgoing.reshape(patches, capacity, rank_width, members),
        "patch",
        split_axis=0,
        concat_axis=0,
        tiled=True,
    )
    cluster_ids = jnp.arange(clusters, dtype=jnp.int32)
    row_targets = far_target.reshape(patches, capacity)
    basis_u = far_basis_u.reshape(patches, capacity, rank_width, 3, CS)

    def add_row(total, inputs):
        row_coeffs, row_basis, row_target = inputs
        per_slot = jnp.einsum(
            "skm,skce->smce", row_coeffs, row_basis, preferred_element_type=jnp.float32
        )
        one_hot = (row_target[None, :] == cluster_ids[:, None]).astype(jnp.float32)
        placed = jnp.einsum("ts,smce->mcte", one_hot, per_slot, precision=lax.Precision.HIGHEST)
        return (total + placed, None)

    far_stress, _ = lax.scan(
        add_row, jnp.zeros((members, 3, clusters, CS), jnp.float32), (arrived, basis_u, row_targets)
    )
    partial_value = (near_stress + far_stress).reshape(members, 3, row_cells)
    summed = lax.psum(partial_value, "col")
    own_stress = lax.dynamic_slice_in_dim(
        summed, lax.axis_index("col") * member_share, member_share, 0
    )
    own_velocity = lax.dynamic_slice_in_dim(
        velocity, lax.axis_index("col") * member_share, member_share, 0
    )
    direct_effect = friction[0][None, :]
    evolve_effect = friction[1][None, :]
    slip_length = friction[2][None, :]
    slip_speed = jnp.sqrt(jnp.sum(own_velocity * own_velocity, axis=1) + speed_floor)
    state_rate = 1.0 - slip_speed * state / slip_length
    pulled = evolve_effect * state_rate / (state * slip_speed)
    velocity_rate = (-own_stress - pulled[:, None, :] * own_velocity) / (
        direct_effect / slip_speed + damping
    )[:, None, :]
    return velocity_rate


def solution(mesh):
    return jax.shard_map(
        shards,
        mesh=mesh,
        in_specs=(
            P("runs", None, "patch"),
            P(("runs", "col"), "patch"),
            P("runs", "patch"),
            P("patch", "col"),
            P("patch", "col", None, None),
            P("col", "patch", None),
            P("col", "patch", None),
            P("col", "patch", None, None, None),
            P("col", "patch", None, None),
            P("col", "patch", None, None, None, None),
        ),
        out_specs=P(("runs", "col"), None, "patch"),
        check_vma=False,
    )
```

profile of v0, /device:TPU:10, one launch (start us, length us, event | category | flops | bytes accessed | tf_op | source)
XLA Modules:
  0.0 482.2 jit_solution(13258005821989255921)
XLA Ops:
  6.5 6.7 %copy.70 = f32[256,3,2048]{0,2,1:T(8,128)} copy(f32[256,3,2048]{2,0,1:T(8,128)} %param.12) | data formatting | bytes 12582912 | tf_op args[0]
  13.2 4.8 %convert_element_type.7 = bf16[256,3,2048]{0,2,1:T(8,128)(2,1)} convert(f32[256,3,2048]{0,2,1:T(8,128)} %copy.70) | non-fusion elementwise | flops 1572864 | bytes 9437184 | tf_op jit(solution)/shard_map/convert_element_type | solution.py:52
  18.1 3.9 reshape.126
  22.4 2.6 fusion.24
  25.0 1.6 broadcast_in_dim.38
  26.6 8.1 %scatter_fusion = bf16[128,32,256]{2,1,0:T(8,128)(2,1)} fusion(bf16[128,32,256]{2,1,0:T(8,128)(2,1)} %broadcast_in_dim.38, s32[64]{0:T(128)S(1)} %fusion.29, bf16[64,32,256]{2,1,0:T(8,128)(2,1)S(1)} %bitcast.70), kind=kCustom, calls=%fused_computation.1 | custom fusion | bytes 3145984 | tf_op jit(solution)/shard_map/scatter | solution.py:71
  34.7 5.0 %all-to-all-start = ((bf16[4,32,32,256]{3,2,1,0:T(8,128)(2,1)}), bf16[4,32,32,256]{3,2,1,0:T(8,128)(2,1)}, u32[]{:S(2)}, u32[]{:S(2)}) async-start(bf16[4,32,32,256]{3,2,1,0:T(8,128)(2,1)} %bitcast.15), calls=%async_computation | async-start | bytes 4194304 | tf_op jit(solution)/shard_map/all_to_all | solution.py:74
  39.7 2.0 collective-permute-start
  41.8 3.7 collective-permute-start.1
  45.8 24.6 %reshape.124 = bf16[16,2,3,128,3,128]{5,4,3,2,1,0:T(4,128)(2,1)} reshape(bf16[16,2,384,384]{3,2,1,0:T(8,128)(2,1)} %param.16) | data formatting | bytes 18874368 | tf_op jit(solution)/shard_map/reshape | solution.py:58
  70.4 3.9 reshape.130
  74.3 3.0 copy.79
  77.3 106.9 %while.11 = (s32[]{:T(128)}, f32[256,3,16,128]{3,2,1,0:T(8,128)}, bf16[4,32,32,256]{3,2,1,0:T(8,128)(2,1)}, bf16[4,32,32,3,128]{4,2,3,1,0:T(8,128)(2,1)S(1)}, s32[4,32]{1,0:T(4,128)}, /*index=5*/s32[]{:T(128)}, s32[]{:T(128)}) while((s32[]{:T(128)}, f32[256,3,16,128]{3,2,1,0:T(8,128)}, bf16[4,32,32,256]{3,2,1,0:T(8,128)(2,1)}, ...), condition=%wide.region_2.3_spmd.clone, body=%wide.region_1.2_spmd.clone.sunk | while | flops 808452608 | bytes 39060952 | solution.py:94
  77.3 7.4 %fusion.42 = f32[32,256,3,128]{3,1,2,0:T(8,128)} fusion(bf16[4,32,32,3,128]{4,2,3,1,0:T(8,128)(2,1)S(1)} %get-tuple-element.138, s32[]{:T(128)} %get-tuple-element.128, bf16[4,32,32,256]{3,2,1,0:T(8,128)(2,1)} %get-tuple-element.137), kind=kOutput, calls=%fused_computation.6.clone.1 | convolution fusion | flops 201326592 | bytes 13894656 | tf_op jit(solution)/shard_map/while/body/eval_jaxpr/skm,skce->smce/dot_general | solution.py:87
  85.3 18.0 %bitcast_add_fusion.3 = f32[256,3,16,128]{3,2,1,0:T(8,128)} fusion(f32[256,3,16,128]{3,2,1,0:T(8,128)} %get-tuple-element.129, pred[]{:T(512)S(6)} %compare.3, f32[32,256,3,128]{3,1,2,0:T(8,128)} %fusion.42, s32[32]{0:T(128)S(1)} %fusion.43), kind=kOutput, calls=%fused_computation.5.clone.1 | convolution fusion | flops 607126016 | bytes 25165952 | tf_op jit(solution)/shard_map/while/body/eval_jaxpr/ts,smce->mcte/dot_general | solution.py:91
  103.3 7.4 %fusion.42 = f32[32,256,3,128]{3,1,2,0:T(8,128)} fusion(bf16[4,32,32,3,128]{4,2,3,1,0:T(8,128)(2,1)S(1)} %get-tuple-element.138, s32[]{:T(128)} %get-tuple-element.128, bf16[4,32,32,256]{3,2,1,0:T(8,128)(2,1)} %get-tuple-element.137), kind=kOutput, calls=%fused_computation.6.clone.1 | convolution fusion | flops 201326592 | bytes 13894656 | tf_op jit(solution)/shard_map/while/body/eval_jaxpr/skm,skce->smce/dot_general | solution.py:87
  111.3 18.9 %bitcast_add_fusion.3 = f32[256,3,16,128]{3,2,1,0:T(8,128)} fusion(f32[256,3,16,128]{3,2,1,0:T(8,128)} %get-tuple-element.129, pred[]{:T(512)S(6)} %compare.3, f32[32,256,3,128]{3,1,2,0:T(8,128)} %fusion.42, s32[32]{0:T(128)S(1)} %fusion.43), kind=kOutput, calls=%fused_computation.5.clone.1 | convolution fusion | flops 607126016 | bytes 25165952 | tf_op jit(solution)/shard_map/while/body/eval_jaxpr/ts,smce->mcte/dot_general | solution.py:91
  130.2 7.4 %fusion.42 = f32[32,256,3,128]{3,1,2,0:T(8,128)} fusion(bf16[4,32,32,3,128]{4,2,3,1,0:T(8,128)(2,1)S(1)} %get-tuple-element.138, s32[]{:T(128)} %get-tuple-element.128, bf16[4,32,32,256]{3,2,1,0:T(8,128)(2,1)} %get-tuple-element.137), kind=kOutput, calls=%fused_computation.6.clone.1 | convolution fusion | flops 201326592 | bytes 13894656 | tf_op jit(solution)/shard_map/while/body/eval_jaxpr/skm,skce->smce/dot_general | solution.py:87
  138.3 18.9 %bitcast_add_fusion.3 = f32[256,3,16,128]{3,2,1,0:T(8,128)} fusion(f32[256,3,16,128]{3,2,1,0:T(8,128)} %get-tuple-element.129, pred[]{:T(512)S(6)} %compare.3, f32[32,256,3,128]{3,1,2,0:T(8,128)} %fusion.42, s32[32]{0:T(128)S(1)} %fusion.43), kind=kOutput, calls=%fused_computation.5.clone.1 | convolution fusion | flops 607126016 | bytes 25165952 | tf_op jit(solution)/shard_map/while/body/eval_jaxpr/ts,smce->mcte/dot_general | solution.py:91
  157.2 7.4 %fusion.42 = f32[32,256,3,128]{3,1,2,0:T(8,128)} fusion(bf16[4,32,32,3,128]{4,2,3,1,0:T(8,128)(2,1)S(1)} %get-tuple-element.138, s32[]{:T(128)} %get-tuple-element.128, bf16[4,32,32,256]{3,2,1,0:T(8,128)(2,1)} %get-tuple-element.137), kind=kOutput, calls=%fused_computation.6.clone.1 | convolution fusion | flops 201326592 | bytes 13894656 | tf_op jit(solution)/shard_map/while/body/eval_jaxpr/skm,skce->smce/dot_general | solution.py:87
  165.2 18.9 %bitcast_add_fusion.3 = f32[256,3,16,128]{3,2,1,0:T(8,128)} fusion(f32[256,3,16,128]{3,2,1,0:T(8,128)} %get-tuple-element.129, pred[]{:T(512)S(6)} %compare.3, f32[32,256,3,128]{3,1,2,0:T(8,128)} %fusion.42, s32[32]{0:T(128)S(1)} %fusion.43), kind=kOutput, calls=%fused_computation.5.clone.1 | convolution fusion | flops 607126016 | bytes 25165952 | tf_op jit(solution)/shard_map/while/body/eval_jaxpr/ts,smce->mcte/dot_general | solution.py:91
  184.1 6.7 %copy.80 = f32[256,3,16,128]{0,3,2,1:T(8,128)} copy(f32[256,3,16,128]{3,2,1,0:T(8,128)} %get-tuple-element.37) | data formatting | bytes 12582912 | tf_op jit(solution)/shard_map/while | solution.py:94
  190.8 8.6 %pad_maximum_fusion = bf16[256,3,6144]{0,2,1:T(8,128)(2,1)} fusion(bf16[256,3,2048]{0,2,1:T(8,128)(2,1)} %collective-permute-done.1, bf16[256,3,2048]{0,2,1:T(8,128)(2,1)} %convert_element_type.7, bf16[256,3,2048]{0,2,1:T(8,128)(2,1)} %collective-permute-done), kind=kLoop, calls=%fused_computation.17 | loop fusion | flops 28311552 | bytes 18874368 | tf_op jit(solution)/shard_map/concatenate | solution.py:19
  199.4 12.6 %copy.72 = bf16[256,3,48,128]{3,0,2,1:T(8,128)(2,1)} copy(bf16[256,3,48,128]{0,3,2,1:T(8,128)(2,1)} %bitcast.66) | data formatting | bytes 18874368 | tf_op jit(solution)/shard_map/reshape | solution.py:54
  212.0 7.6 %gather_fusion = bf16[32,256,3,128]{3,1,2,0:T(8,128)(2,1)} fusion(bf16[256,3,48,128]{3,0,2,1:T(8,128)(2,1)} %copy.72, s32[1024]{0:T(1024)S(1)} %pad_clamp_fusion), kind=kCustom, calls=%fused_computation | custom fusion | bytes 12583040 | tf_op jit(solution)/shard_map/jit(_take)/gather | solution.py:57
  219.6 6.2 %copy.73 = bf16[256,3,32,128]{3,0,2,1:T(8,128)(2,1)} copy(bf16[256,3,32,128]{3,0,1,2:T(8,128)(2,1)} %bitcast.67) | data formatting | bytes 12582912 | tf_op jit(solution)/shard_map/jit(_take)/gather | solution.py:57
  225.8 11.7 %fusion.16 = f32[16,256,3,128,1,1]{1,3,5,2,0,4:T(8,128)} fusion(bf16[16,2,3,128,3,128]{5,4,3,2,1,0:T(4,128)(2,1)} %reshape.124, bf16[256,3,16,2,128]{4,0,3,2,1:T(8,128)(2,1)} %bitcast.69, pred[16,2]{1,0:T(8,128)(4,1)S(1)} %copy.69), kind=kOutput, calls=%fused_computation.18 | convolution fusion | flops 2419064832 | bytes 22020128 | tf_op jit(solution)/shard_map/mctje,tjadce->matd/dot_general | solution.py:59
  237.5 8.6 %bitcast_add_fusion.1 = f32[256,3,16,128]{0,3,2,1:T(8,128)} fusion(f32[256,3,16,128]{0,3,2,1:T(8,128)} %copy.80, f32[16,256,3,128,1,1]{1,3,5,2,0,4:T(8,128)} %fusion.16), kind=kLoop, calls=%fused_computation.20 | loop fusion | flops 1572864 | bytes 18874368 | tf_op jit(solution)/shard_map/add | solution.py:97
  246.2 2.9 multiply_reduce_fusion
  252.4 215.9 %all-reduce.2.cloned.1.call-done = f32[256,3,2048]{0,2,1:T(8,128)} async-done(((f32[256,3,2048]{0,2,1:T(8,128)}), f32[256,3,2048]{0,2,1:T(8,128)}) %all-reduce.2.cloned.1.call-update) | async-done | bytes 6291472 | tf_op jit(solution)/shard_map/psum | solution.py:98
  468.3 5.1 %subtract_divide_fusion = f32[64,3,2048]{0,2,1:T(8,128)S(1)} fusion(f32[256,3,2048]{0,2,1:T(8,128)} %all-reduce.2.cloned.1.call-done, s32[]{:T(128)S(6)} %select_n.45, f32[256,3,2048]{0,2,1:T(8,128)} %copy.70, f32[64,2048]{0,1:T(8,128)} %copy.84, f32[64,2048]{0,1:T(8,128)} %copy.83), kind=kLoop, calls=%fused_computation.26 | loop fusion | flops 1572864 | bytes 5767172 | tf_op jit(solution)/shard_map/div | solution.py:111
  473.4 2.0 copy.85
  (38 shorter events, 6.7 us)
Async XLA Ops:
  13.2 8.8 %copy-start.3 = (s32[1,16,4]{1,2,0:T(4,128)S(1)}, s32[1,16,4]{1,2,0:T(4,128)}, u32[]{:S(2)}) copy-start(s32[1,16,4]{1,2,0:T(4,128)} %param.18) | copy-start | bytes 772
  13.2 9.0 %copy-start.4 = (s32[1,16,4]{1,2,0:T(4,128)S(1)}, s32[1,16,4]{1,2,0:T(4,128)}, u32[]{:S(2)}) copy-start(s32[1,16,4]{1,2,0:T(4,128)} %param.17) | copy-start | bytes 772
  25.0 20.5 %copy-start.5 = (s32[16,2]{0,1:T(2,128)S(1)}, s32[16,2]{0,1:T(2,128)}, u32[]{:S(2)}) copy-start(s32[16,2]{0,1:T(2,128)} %param.15) | copy-start | bytes 388
  34.7 42.5 %all-to-all-start = ((bf16[4,32,32,256]{3,2,1,0:T(8,128)(2,1)}), bf16[4,32,32,256]{3,2,1,0:T(8,128)(2,1)}, u32[]{:S(2)}, u32[]{:S(2)}) async-start(bf16[4,32,32,256]{3,2,1,0:T(8,128)(2,1)} %bitcast.15), calls=%async_computation | async-start | bytes 4194304 | tf_op jit(solution)/shard_map/all_to_all | solution.py:74
  39.7 428.6 %all-reduce.2.cloned.1.call-start = ((), (), s32[]{:S(2)}) async-start(), calls=%async_computation.1 | async-start | bytes 12582912 | tf_op jit(solution)/shard_map/psum | solution.py:98
  39.7 151.1 %collective-permute-start = (bf16[256,3,2048]{0,2,1:T(8,128)(2,1)}, bf16[256,3,2048]{0,2,1:T(8,128)(2,1)}, u32[]{:S(2)}, u32[]{:S(2)}) collective-permute-start(bf16[256,3,2048]{0,2,1:T(8,128)(2,1)} %convert_element_type.7), channel_id=1, source_target_pairs={{0,4},{4,8},{8,12},{1,5},{5,9},{9,13},{2,6},{6,10},{10,14},{3,7},{... | collective-permute-start | bytes 9437192 | tf_op jit(solution)/shard_map/ppermute | solution.py:21
  41.8 149.0 %collective-permute-start.1 = (bf16[256,3,2048]{0,2,1:T(8,128)(2,1)}, bf16[256,3,2048]{0,2,1:T(8,128)(2,1)}, u32[]{:S(2)}, u32[]{:S(2)}) collective-permute-start(bf16[256,3,2048]{0,2,1:T(8,128)(2,1)} %convert_element_type.7), channel_id=1, source_target_pairs={{4,0},{8,4},{12,8},{5,1},{9,5},{13,9},{6,2},{10,6},{14,10},{7,3},{... | collective-permute-start | bytes 9437192 | tf_op jit(solution)/shard_map/ppermute | solution.py:23
  45.8 24.6 %copy-start = (bf16[1,1,4,32,32,384]{5,4,3,2,1,0:T(8,128)(2,1)S(1)}, bf16[1,1,4,32,32,384]{5,4,3,2,1,0:T(8,128)(2,1)}, u32[]{:S(2)}) copy-start(bf16[1,1,4,32,32,384]{5,4,3,2,1,0:T(8,128)(2,1)} %param.21) | copy-start | bytes 9437188
  246.1 3.3 copy-start.2
  246.1 3.3 copy-start.1
Sparse Core Ops, SparseCore 0:
  246.3 221.9 all-reduce.1
where the time goes:
time: 488 us; the launch traced here: 482 us
  waiting for transfers between devices  216 us (44%)
  matrix products  118 us (24%)
  local copies, waits for them, and re-layouts  93.1 us (19%)
  other arithmetic  30.4 us (6%)
  between operations  13.6 us (3%)
  starting transfers between devices  10.7 us (2%)
    psum x1, waiting for transfers between devices, shards(): summed = lax.psum(partial_value, 'col')  216 us
    dot_general x4, matrix products, add_row(): jnp.einsum('ts,smce->mcte', one_hot, per_slot, precision=lax.Precision.HI...  74.7 us
    dot_general x4, matrix products, add_row(): jnp.einsum('skm,skce->smce', row_coeffs, row_basis, preferred_element_typ...  29.4 us
    reshape x1, local copies, waits for them, and re-layouts, shards(): blocks = near_block.reshape(clusters, near_count, 3, CS, 3, CS)  24.6 us
    gather x2, local copies, waits for them, and re-layouts, shards(): jnp.take(extended, local_index, axis=2)  13.8 us
    reshape x1, local copies, waits for them, and re-layouts, shards(): extended = extended.reshape(members, 3, 3 * clusters, CS)  12.6 us
    dot_general x1, matrix products, shards(): jnp.einsum('mctje,tjadce->matd', gathered, blocks, preferred_element_type...  11.7 us
    unnamed x15, local copies, waits for them, and re-layouts  9.76 us
  transfers between devices with their start and end apart: 4, of which 1 were waited for; matrix products, arithmetic and copies ran while one was open for 31% of the time, Pallas kernels for 0%

commit v1 on v0

v1 whole, which is shorter than its diff:
```python
import functools
import jax
import jax.numpy as jnp
from jax import lax
from jax.experimental import pallas as pl
from jax.experimental.pallas import tpu as pltpu
from jax.sharding import PartitionSpec as P

CS = 128
CHUNKS = 2
GROUP = 8
MIB = 1 << 20

damping = 0.5
speed_floor = 0.25

NT = (((1,), (1,)), ((), ()))
TN = (((0,), (0,)), ((), ()))


def source_kernel(far_count, rank_width, dest_ref, rank_ref, vel_ref, basis_ref, own_ref, coef_ref):
    g = pl.program_id(0)
    members = own_ref.shape[1]
    for c in range(3):
        part = vel_ref[c].reshape(members, CS).astype(jnp.bfloat16)
        own_ref[0, :, c * CS : (c + 1) * CS] = part
    raw = lax.dot_general(basis_ref[0], own_ref[0], NT, preferred_element_type=jnp.float32)
    rows = lax.broadcasted_iota(jnp.int32, (rank_width, members), 0)
    for j in range(far_count):
        block = raw[j * rank_width : (j + 1) * rank_width]
        block = jnp.where(rows < rank_ref[g * far_count + j], block, 0.0)
        coef_ref[dest_ref[g * far_count + j]] = block.astype(jnp.bfloat16)


def source_step(chunk, velocity, basis_v, dest, rank):
    _, shares, _, sub, row_cells = velocity.shape
    members = shares * sub
    clusters = row_cells // CS
    far_count = dest.shape[0] // clusters
    rank_width = basis_v.shape[1] // far_count
    width = basis_v.shape[2]

    def call(slots):
        return pl.pallas_call(
            functools.partial(source_kernel, far_count, rank_width),
            grid_spec=pltpu.PrefetchScalarGridSpec(
                num_scalar_prefetch=2,
                grid=(clusters,),
                in_specs=[
                    pl.BlockSpec((3, shares, None, sub, CS), lambda g, *_: (0, 0, chunk, 0, g)),
                    pl.BlockSpec((1, far_count * rank_width, width), lambda g, *_: (g, 0, 0)),
                ],
                out_specs=[
                    pl.BlockSpec((1, members, width), lambda g, *_: (g, 0, 0)),
                    pl.BlockSpec((slots, rank_width, members), lambda g, *_: (0, 0, 0)),
                ],
            ),
            out_shape=[
                jax.ShapeDtypeStruct((clusters, members, width), jnp.bfloat16),
                jax.ShapeDtypeStruct((slots, rank_width, members), jnp.bfloat16),
            ],
            compiler_params=pltpu.CompilerParams(vmem_limit_bytes=24 * MIB),
            cost_estimate=pl.CostEstimate(
                flops=2 * clusters * far_count * rank_width * width * members,
                bytes_accessed=8 * MIB,
                transcendentals=0,
            ),
            name="source",
        )(dest, rank, velocity, basis_v)

    return call


def target_kernel(
    near_count, rank_width, src_ref, target_ref,
    left_ref, own_ref, right_ref, block_ref, coef_ref, basis_ref,
    out_ref, cells, acc, picked_c, picked_u, slot_list, slot_count, sems,
):
    t = pl.program_id(0)
    clusters = own_ref.shape[0]
    slots = coef_ref.shape[0]
    shares, _, sub, _ = out_ref.shape

    @pl.when(t == 0)
    def _():
        copies = [
            pltpu.make_async_copy(ref, cells.at[pl.ds(i * clusters, clusters)], sems.at[i])
            for i, ref in enumerate((left_ref, own_ref, right_ref))
        ]
        for copy in copies:
            copy.start()

        def clear(i, carry):
            slot_count[i] = 0
            return carry

        lax.fori_loop(0, clusters, clear, 0)

        def place(s, carry):
            goal = target_ref[s]

            @pl.when(goal >= 0)
            def _():
                at = slot_count[goal]
                slot_list[goal * slots + at] = s
                slot_count[goal] = at + 1

            return carry

        lax.fori_loop(0, slots, place, 0)
        for copy in copies:
            copy.wait()

    total = None
    for j in range(near_count):
        cell = cells[src_ref[t * near_count + j]]
        part = lax.dot_general(cell, block_ref[0, j], NT, preferred_element_type=jnp.float32)
        total = part if total is None else total + part
    acc[...] = total
    count = slot_count[t]

    def group(i, carry):
        for j in range(GROUP):
            at = i * GROUP + j
            live = at < count
            s = slot_list[t * slots + jnp.where(live, at, 0)]
            s = jnp.where(live, s, 0)
            piece = pl.ds(j * rank_width, rank_width)
            coef = coef_ref[s]
            picked_c[piece, :] = jnp.where(live, coef, jnp.zeros_like(coef))
            picked_u[piece, :] = basis_ref[s]
        acc[...] += lax.dot_general(
            picked_c[...], picked_u[...], TN, preferred_element_type=jnp.float32
        )
        return carry

    lax.fori_loop(0, (count + GROUP - 1) // GROUP, group, 0)
    for d in range(shares):
        for c in range(3):
            out_ref[d, c] = acc[d * sub : (d + 1) * sub, c * CS : (c + 1) * CS].astype(jnp.bfloat16)


def target_step(shares, src, target, left, own, right, blocks, coef, basis_u):
    clusters, members, width = own.shape
    near_count = blocks.shape[1]
    slots, rank_width, _ = coef.shape
    sub = members // shares
    whole = lambda t, *_: (0, 0, 0)
    return pl.pallas_call(
        functools.partial(target_kernel, near_count, rank_width),
        grid_spec=pltpu.PrefetchScalarGridSpec(
            num_scalar_prefetch=2,
            grid=(clusters,),
            in_specs=[
                pl.BlockSpec(memory_space=pl.ANY),
                pl.BlockSpec(memory_space=pl.ANY),
                pl.BlockSpec(memory_space=pl.ANY),
                pl.BlockSpec((1, near_count, width, width), lambda t, *_: (t, 0, 0, 0)),
                pl.BlockSpec((slots, rank_width, members), whole),
                pl.BlockSpec((slots, rank_width, width), whole),
            ],
            out_specs=pl.BlockSpec((shares, 3, sub, CS), lambda t, *_: (0, 0, 0, t)),
            scratch_shapes=[
                pltpu.VMEM((3 * clusters, members, width), jnp.bfloat16),
                pltpu.VMEM((members, width), jnp.float32),
                pltpu.VMEM((GROUP * rank_width, members), jnp.bfloat16),
                pltpu.VMEM((GROUP * rank_width, width), jnp.bfloat16),
                pltpu.SMEM((clusters * slots,), jnp.int32),
                pltpu.SMEM((clusters,), jnp.int32),
                pltpu.SemaphoreType.DMA((3,)),
            ],
        ),
        out_shape=jax.ShapeDtypeStruct((shares, 3, sub, clusters * CS), jnp.bfloat16),
        compiler_params=pltpu.CompilerParams(vmem_limit_bytes=36 * MIB),
        cost_estimate=pl.CostEstimate(
            flops=2 * clusters * members * width * (near_count * width + GROUP * rank_width),
            bytes_accessed=24 * MIB,
            transcendentals=0,
        ),
        name="target",
    )(src, target, left, own, right, blocks, coef, basis_u)


def law_kernel(chunks, col_ref, *refs):
    parts = refs[:chunks]
    vel_ref, state_ref, friction_ref, out_ref = refs[chunks:]
    sub = parts[0].shape[2]
    for h in range(chunks):
        rows = slice(h * sub, (h + 1) * sub)
        velocity = [vel_ref[c, rows, :] for c in range(3)]
        speed = jnp.sqrt(
            velocity[0] * velocity[0] + velocity[1] * velocity[1] + velocity[2] * velocity[2] + speed_floor
        )
        state = state_ref[rows, :]
        state_rate = 1.0 - speed * state / friction_ref[2:3, :]
        pulled = friction_ref[1:2, :] * state_rate / (state * speed)
        below = friction_ref[0:1, :] / speed + damping
        for c in range(3):
            stress = jnp.sum(parts[h][:, c].astype(jnp.float32), axis=0)
            out_ref[c, rows, :] = (-stress - pulled * velocity[c]) / below


def law_step(col, parts, velocity, state, friction):
    member_share, row_cells = state.shape
    chunks = len(parts)
    shares, _, sub, _ = parts[0].shape
    tile = min(512, row_cells)
    return pl.pallas_call(
        functools.partial(law_kernel, chunks),
        grid_spec=pltpu.PrefetchScalarGridSpec(
            num_scalar_prefetch=1,
            grid=(row_cells // tile,),
            in_specs=[pl.BlockSpec((shares, 3, sub, tile), lambda e, col: (0, 0, 0, e))] * chunks
            + [
                pl.BlockSpec((3, member_share, tile), lambda e, col: (0, col[0], e)),
                pl.BlockSpec((member_share, tile), lambda e, col: (0, e)),
                pl.BlockSpec((3, tile), lambda e, col: (0, e)),
            ],
            out_specs=pl.BlockSpec((3, member_share, tile), lambda e, col: (0, 0, e)),
        ),
        out_shape=jax.ShapeDtypeStruct((3, member_share, row_cells), jnp.float32),
        compiler_params=pltpu.CompilerParams(vmem_limit_bytes=24 * MIB),
        cost_estimate=pl.CostEstimate(flops=MIB * 16, bytes_accessed=8 * MIB, transcendentals=0),
        name="law",
    )(col, *parts, velocity, state, friction)


def shards(
    velocity,
    state,
    friction,
    near_src,
    near_block,
    far_dest,
    far_rank,
    far_basis_v,
    far_target,
    far_basis_u,
):
    members, _, row_cells = velocity.shape
    clusters = row_cells // CS
    near_count = near_src.shape[1]
    far_count = far_dest.shape[2]
    rank_width, width = far_basis_v.shape[3:]
    patches = lax.axis_size("patch")
    shares = lax.axis_size("col")
    capacity = far_target.shape[3]
    slots = patches * capacity
    member_share = state.shape[0]
    sub = member_share // CHUNKS
    planes = jnp.transpose(velocity, (1, 0, 2))
    split = planes.reshape(3, shares, CHUNKS, sub, row_cells)
    basis_v = far_basis_v.reshape(clusters, far_count * rank_width, width)
    basis_u = far_basis_u.reshape(slots, rank_width, width)
    blocks = near_block
    dest = far_dest.reshape(-1)
    rank = far_rank.reshape(-1)
    target = far_target.reshape(-1)
    first = lax.axis_index("patch") * clusters - clusters
    src = (near_src - first).reshape(-1)
    ends = patches - 1
    up = [(i, i + 1) for i in range(ends)]
    down = [(i + 1, i) for i in range(ends)]
    parts = []
    for h in range(CHUNKS):
        own, coef = source_step(h, split, basis_v, dest, rank)(slots)
        left = lax.ppermute(own, "patch", up)
        right = lax.ppermute(own, "patch", down)
        arrived = lax.all_to_all(coef, "patch", split_axis=0, concat_axis=0, tiled=True)
        partial = target_step(shares, src, target, left, own, right, blocks, arrived, basis_u)
        parts.append(lax.all_to_all(partial, "col", split_axis=0, concat_axis=0, tiled=True))
    col = lax.axis_index("col").reshape(1).astype(jnp.int32)
    rate = law_step(col, parts, planes, state, friction)
    return jnp.transpose(rate, (1, 0, 2))


def solution(mesh):
    return jax.shard_map(
        shards,
        mesh=mesh,
        in_specs=(
            P("runs", None, "patch"),
            P(("runs", "col"), "patch"),
            P("runs", "patch"),
            P("patch", "col"),
            P("patch", "col", None, None),
            P("col", "patch", None),
            P("col", "patch", None),
            P("col", "patch", None, None, None),
            P("col", "patch", None, None),
            P("col", "patch", None, None, None, None),
        ),
        out_specs=P(("runs", "col"), None, "patch"),
        check_vma=False,
    )
```

time: 488 us -> 164 us (0.34)
  the two profiles are of different devices: /device:TPU:10 before, /device:TPU:1 now
where the time goes in v1:
time: 164 us; the launch traced here: 162 us
  waiting for transfers between devices  62.8 us (38%)
  Pallas kernels  51.6 us (31%)
  starting transfers between devices  29 us (18%)
  local copies, waits for them, and re-layouts  19 us (12%)
    pallas_call x2, Pallas kernels, target_step(): pl.pallas_call(functools.partial(target_kernel, near_count, rank_width),...  36.2 us
    all_to_all x2, waiting for transfers between devices, shards(): lax.all_to_all(partial, 'col', split_axis=0, concat_axis=0, tiled=True)  31.2 us
    unnamed x32, local copies, waits for them, and re-layouts  18.5 us
    ppermute x2, waiting for transfers between devices, shards(): right = lax.ppermute(own, 'patch', down)  16.8 us
    all_to_all x2, waiting for transfers between devices, shards(): lax.all_to_all(coef, 'patch', split_axis=0, concat_axis=0, tiled=True)  13.9 us
    pallas_call x2, Pallas kernels, call(): pl.pallas_call(functools.partial(source_kernel, far_count, rank_width), g...  11.3 us
    all_to_all x2, starting transfers between devices, shards(): lax.all_to_all(partial, 'col', split_axis=0, concat_axis=0, tiled=True)  8.51 us
    all_to_all x2, starting transfers between devices, shards(): lax.all_to_all(coef, 'patch', split_axis=0, concat_axis=0, tiled=True)  8.47 us
  transfers between devices with their start and end apart: 8, of which 4 were waited for; matrix products, arithmetic and copies ran while one was open for 0% of the time, Pallas kernels for 25%

profile of v1, /device:TPU:1, one launch (start us, length us, event | category | flops | bytes accessed | tf_op | source)
XLA Modules:
  0.0 162.5 jit_solution(13292372318373264480)
XLA Ops:
  0.0 0.8 copy.15
  0.8 0.8 copy.16
  1.6 0.1 reshape.28.rank_ref
  1.7 2.8 %copy-done = f32[256,3,2048]{2,0,1:T(8,128)S(1)} copy-done((f32[256,3,2048]{2,0,1:T(8,128)S(1)}, f32[256,3,2048]{2,0,1:T(8,128)}, u32[]{:S(2)}) %copy-start) | copy-done | bytes 6291480
  4.5 1.4 copy-done.6
  5.9 6.9 %source.3 = (bf16[16,128,384]{2,1,0:T(8,128)(2,1)}, bf16[128,32,128]{2,1,0:T(8,128)(2,1)}) custom-call(s32[64]{0:T(128)S(1)} %reshape.27.dest_ref, s32[64]{0:T(128)S(1)} %reshape.28.rank_ref, f32[3,4,2,32,2048]{4,3,2,1,0:T(8,128)S(1)} %bitcast.7, bf16[16,128,384]{2,1,0:T(8,128)(2,1)S(1)} %bitcast.12), custom_call_target="tpu_custom_call" | custom-call | flops 201326592 | bytes 8388608 | tf_op jit(solution)/shard_map/source/pallas_call | solution.py:44
  12.8 2.0 %collective-permute-start.3 = (bf16[16,128,384]{2,1,0:T(8,128)(2,1)}, bf16[16,128,384]{2,1,0:T(8,128)(2,1)}, u32[]{:S(2)}, u32[]{:S(2)}) collective-permute-start(bf16[16,128,384]{2,1,0:T(8,128)(2,1)} %get-tuple-element.11.own_ref), channel_id=1, source_target_pairs={{4,0},{8,4},{12,8},{5,1},{9,5},{13,9},{6,2},{10,6},{14,10},{7,3},{... | collective-permute-start | bytes 4718600 | tf_op jit(solution)/shard_map/ppermute | solution.py:268
  14.8 4.5 %collective-permute-start.2 = (bf16[16,128,384]{2,1,0:T(8,128)(2,1)}, bf16[16,128,384]{2,1,0:T(8,128)(2,1)}, u32[]{:S(2)}, u32[]{:S(2)}) collective-permute-start(bf16[16,128,384]{2,1,0:T(8,128)(2,1)} %get-tuple-element.11.own_ref), channel_id=1, source_target_pairs={{0,4},{4,8},{8,12},{1,5},{5,9},{9,13},{2,6},{6,10},{10,14},{3,7},{... | collective-permute-start | bytes 4718600 | tf_op jit(solution)/shard_map/ppermute | solution.py:267
  19.3 4.2 %all-to-all-start.2 = ((bf16[128,32,128]{2,1,0:T(8,128)(2,1)}), bf16[128,32,128]{2,1,0:T(8,128)(2,1)}, u32[]{:S(2)}, u32[]{:S(2)}) async-start(bf16[128,32,128]{2,1,0:T(8,128)(2,1)} %get-tuple-element.12), calls=%async_computation.2 | async-start | bytes 2097152 | tf_op jit(solution)/shard_map/all_to_all | solution.py:269
  23.5 2.8 %copy-done.1 = f32[256,3,2048]{2,0,1:T(8,128)S(1)} copy-done((f32[256,3,2048]{2,0,1:T(8,128)S(1)}, f32[256,3,2048]{2,0,1:T(8,128)}, u32[]{:S(2)}) %copy-start.1) | copy-done | bytes 6291480
  26.3 1.4 copy-done.7
  27.7 4.4 %source.2 = (bf16[16,128,384]{2,1,0:T(8,128)(2,1)S(1)}, bf16[128,32,128]{2,1,0:T(8,128)(2,1)S(1)}) custom-call(s32[64]{0:T(128)S(1)} %reshape.27.dest_ref, s32[64]{0:T(128)S(1)} %reshape.28.rank_ref, f32[3,4,2,32,2048]{4,3,2,1,0:T(8,128)S(1)} %bitcast.8, bf16[16,128,384]{2,1,0:T(8,128)(2,1)S(1)} %bitcast.13), custom_call_target="tpu_custom_call" | custom-call | flops 201326592 | bytes 8388608 | tf_op jit(solution)/shard_map/source/pallas_call | solution.py:44
  32.1 1.1 copy-done.8
  33.2 1.0 copy-done.10
  34.2 13.9 %all-to-all-done.2.coef_ref = bf16[128,32,128]{2,1,0:T(8,128)(2,1)} async-done(((bf16[128,32,128]{2,1,0:T(8,128)(2,1)}), bf16[128,32,128]{2,1,0:T(8,128)(2,1)}, u32[]{:S(2)}, u32[]{:S(2)}) %all-to-all-start.2) | async-done | bytes 1048608 | tf_op jit(solution)/shard_map/all_to_all | solution.py:269
  48.2 4.2 %all-to-all-start = ((bf16[128,32,128]{2,1,0:T(8,128)(2,1)}), bf16[128,32,128]{2,1,0:T(8,128)(2,1)}, u32[]{:S(2)}, u32[]{:S(2)}) async-start(bf16[128,32,128]{2,1,0:T(8,128)(2,1)} %copy-done.10), calls=%async_computation | async-start | bytes 2097152 | tf_op jit(solution)/shard_map/all_to_all | solution.py:269
  52.5 0.1 copy.14
  52.6 0.1 reshape.25.src_ref
  52.7 18.2 %target.3 = bf16[4,3,32,2048]{3,2,1,0:T(8,128)(2,1)S(1)} custom-call(s32[32]{0:T(128)S(1)} %reshape.25.src_ref, s32[128]{0:T(128)S(1)} %reshape.26.target_ref, bf16[16,128,384]{2,1,0:T(8,128)(2,1)} %collective-permute-done.2.left_ref, bf16[16,128,384]{2,1,0:T(8,128)(2,1)} %get-tuple-element.11.own_ref, ...), custom_call_target="tpu_custom_call" | custom-call | flops 1610612736 | bytes 25165824 | tf_op jit(solution)/shard_map/target/pallas_call | solution.py:149
  70.9 1.1 copy-done.4
  72.0 4.4 %all-to-all-start.3 = ((bf16[4,3,32,2048]{3,2,1,0:T(8,128)(2,1)}), bf16[4,3,32,2048]{3,2,1,0:T(8,128)(2,1)}, u32[]{:S(2)}, u32[]{:S(2)}) async-start(bf16[4,3,32,2048]{3,2,1,0:T(8,128)(2,1)} %copy-done.4), calls=%async_computation.3 | async-start | bytes 3145728 | tf_op jit(solution)/shard_map/all_to_all | solution.py:271
  76.4 1.9 %collective-permute-start.1 = (bf16[16,128,384]{2,1,0:T(8,128)(2,1)}, bf16[16,128,384]{2,1,0:T(8,128)(2,1)S(1)}, u32[]{:S(2)}, u32[]{:S(2)}) collective-permute-start(bf16[16,128,384]{2,1,0:T(8,128)(2,1)} %copy-done.8), channel_id=1, source_target_pairs={{4,0},{8,4},{12,8},{5,1},{9,5},{13,9},{6,2},{10,6},{14,10},{7,3},{... | collective-permute-start | bytes 4718600 | tf_op jit(solution)/shard_map/ppermute | solution.py:268
  78.3 3.6 %collective-permute-start = (bf16[16,128,384]{2,1,0:T(8,128)(2,1)}, bf16[16,128,384]{2,1,0:T(8,128)(2,1)S(1)}, u32[]{:S(2)}, u32[]{:S(2)}) collective-permute-start(bf16[16,128,384]{2,1,0:T(8,128)(2,1)} %copy-done.8), channel_id=1, source_target_pairs={{0,4},{4,8},{8,12},{1,5},{5,9},{9,13},{2,6},{6,10},{10,14},{3,7},{... | collective-permute-start | bytes 4718600 | tf_op jit(solution)/shard_map/ppermute | solution.py:267
  82.0 16.8 %collective-permute-done.1.right_ref = bf16[16,128,384]{2,1,0:T(8,128)(2,1)S(1)} collective-permute-done((bf16[16,128,384]{2,1,0:T(8,128)(2,1)}, bf16[16,128,384]{2,1,0:T(8,128)(2,1)S(1)}, u32[]{:S(2)}, u32[]{:S(2)}) %collective-permute-start.1) | collective-permute-done | bytes 1572896 | tf_op jit(solution)/shard_map/ppermute | solution.py:268
  98.8 0.9 collective-permute-done.left_ref
  99.6 1.4 copy-done.9
  101.0 18.1 %target.2 = bf16[4,3,32,2048]{3,2,1,0:T(8,128)(2,1)S(1)} custom-call(s32[32]{0:T(128)S(1)} %reshape.25.src_ref, s32[128]{0:T(128)S(1)} %reshape.26.target_ref, bf16[16,128,384]{2,1,0:T(8,128)(2,1)S(1)} %collective-permute-done.left_ref, bf16[16,128,384]{2,1,0:T(8,128)(2,1)S(1)} %copy-done.9, bf16[16,128,384]{2,1,0:T(8,128)(2,1)S(1)} %collective-permute-done.1.right_ref, ...), custom_call_target="tpu_custom_call" | custom-call | flops 1610612736 | bytes 25165824 | tf_op jit(solution)/shard_map/target/pallas_call | solution.py:149
  119.1 1.1 copy-done.5
  120.3 4.2 %all-to-all-start.1 = ((bf16[4,3,32,2048]{3,2,1,0:T(8,128)(2,1)}), bf16[4,3,32,2048]{3,2,1,0:T(8,128)(2,1)S(1)}, u32[]{:S(2)}, u32[]{:S(2)}) async-start(bf16[4,3,32,2048]{3,2,1,0:T(8,128)(2,1)} %copy-done.5), calls=%async_computation.1 | async-start | bytes 3145728 | tf_op jit(solution)/shard_map/all_to_all | solution.py:271
  124.4 31.2 %all-to-all-done.1.refs_0_ = bf16[4,3,32,2048]{3,2,1,0:T(8,128)(2,1)S(1)} async-done(((bf16[4,3,32,2048]{3,2,1,0:T(8,128)(2,1)}), bf16[4,3,32,2048]{3,2,1,0:T(8,128)(2,1)S(1)}, u32[]{:S(2)}, u32[]{:S(2)}) %all-to-all-start.1) | async-done | bytes 1572896 | tf_op jit(solution)/shard_map/all_to_all | solution.py:271
  155.6 2.8 %copy-done.2 = f32[256,3,2048]{2,0,1:T(8,128)S(1)} copy-done((f32[256,3,2048]{2,0,1:T(8,128)S(1)}, f32[256,3,2048]{2,0,1:T(8,128)}, u32[]{:S(2)}) %copy-start.2) | copy-done | bytes 6291480
  158.4 4.1 %law.1 = f32[3,64,2048]{2,1,0:T(8,128)} custom-call(s32[1]{0:T(128)} %bitcast.col_ref, bf16[4,3,32,2048]{3,2,1,0:T(8,128)(2,1)S(1)} %all-to-all-done.1.refs_0_, bf16[4,3,32,2048]{3,2,1,0:T(8,128)(2,1)} %all-to-all-done.3.refs_1_, f32[3,256,2048]{2,1,0:T(8,128)S(1)} %bitcast.9, f32[64,2048]{1,0:T(8,128)S(1)} %copy-done.11, f32[3,2048]{1,0:T(4,128)S(1)} %copy-done.12), custom_call_target="tpu_custom_call" | custom-call | flops 16777216 | bytes 8388608 | tf_op jit(solution)/shard_map/law/pallas_call | solution.py:208
  (27 shorter events, 0.2 us)
Async XLA Ops:
  1.7 2.8 %copy-start = (f32[256,3,2048]{2,0,1:T(8,128)S(1)}, f32[256,3,2048]{2,0,1:T(8,128)}, u32[]{:S(2)}) copy-start(f32[256,3,2048]{2,0,1:T(8,128)} %param.10) | copy-start | bytes 18874372
  4.5 1.4 copy-start.6
  12.8 39.9 %collective-permute-start.3 = (bf16[16,128,384]{2,1,0:T(8,128)(2,1)}, bf16[16,128,384]{2,1,0:T(8,128)(2,1)}, u32[]{:S(2)}, u32[]{:S(2)}) collective-permute-start(bf16[16,128,384]{2,1,0:T(8,128)(2,1)} %get-tuple-element.11.own_ref), channel_id=1, source_target_pairs={{4,0},{8,4},{12,8},{5,1},{9,5},{13,9},{6,2},{10,6},{14,10},{7,3},{... | collective-permute-start | bytes 4718600 | tf_op jit(solution)/shard_map/ppermute | solution.py:268
  14.8 37.9 %collective-permute-start.2 = (bf16[16,128,384]{2,1,0:T(8,128)(2,1)}, bf16[16,128,384]{2,1,0:T(8,128)(2,1)}, u32[]{:S(2)}, u32[]{:S(2)}) collective-permute-start(bf16[16,128,384]{2,1,0:T(8,128)(2,1)} %get-tuple-element.11.own_ref), channel_id=1, source_target_pairs={{0,4},{4,8},{8,12},{1,5},{5,9},{9,13},{2,6},{6,10},{10,14},{3,7},{... | collective-permute-start | bytes 4718600 | tf_op jit(solution)/shard_map/ppermute | solution.py:267
  19.3 28.9 %all-to-all-start.2 = ((bf16[128,32,128]{2,1,0:T(8,128)(2,1)}), bf16[128,32,128]{2,1,0:T(8,128)(2,1)}, u32[]{:S(2)}, u32[]{:S(2)}) async-start(bf16[128,32,128]{2,1,0:T(8,128)(2,1)} %get-tuple-element.12), calls=%async_computation.2 | async-start | bytes 2097152 | tf_op jit(solution)/shard_map/all_to_all | solution.py:269
  23.5 2.8 %copy-start.1 = (f32[256,3,2048]{2,0,1:T(8,128)S(1)}, f32[256,3,2048]{2,0,1:T(8,128)}, u32[]{:S(2)}) copy-start(f32[256,3,2048]{2,0,1:T(8,128)} %param.10) | copy-start | bytes 18874372
  26.3 1.4 copy-start.7
  27.7 25.0 %copy-start.3 = (bf16[1,1,4,32,32,384]{5,4,3,2,1,0:T(8,128)(2,1)S(1)}, bf16[1,1,4,32,32,384]{5,4,3,2,1,0:T(8,128)(2,1)}, u32[]{:S(2)}) copy-start(bf16[1,1,4,32,32,384]{5,4,3,2,1,0:T(8,128)(2,1)} %param.19) | copy-start | bytes 9437188
  32.1 1.1 copy-start.8
  33.2 1.0 copy-start.10
  34.2 18.2 %copy-start.13 = (s32[1,1,4,32]{3,2,1,0:T(4,128)S(1)}, s32[1,1,4,32]{3,2,1,0:T(4,128)}, u32[]{:S(2)}) copy-start(s32[1,1,4,32]{3,2,1,0:T(4,128)} %param.18) | copy-start | bytes 1540
  34.2 18.3 %copy-start.14 = (s32[16,2]{0,1:T(2,128)S(1)}, s32[16,2]{0,1:T(2,128)}, u32[]{:S(2)}) copy-start(s32[16,2]{0,1:T(2,128)} %param.13) | copy-start | bytes 388
  48.2 23.9 %all-to-all-start = ((bf16[128,32,128]{2,1,0:T(8,128)(2,1)}), bf16[128,32,128]{2,1,0:T(8,128)(2,1)}, u32[]{:S(2)}, u32[]{:S(2)}) async-start(bf16[128,32,128]{2,1,0:T(8,128)(2,1)} %copy-done.10), calls=%async_computation | async-start | bytes 2097152 | tf_op jit(solution)/shard_map/all_to_all | solution.py:269
  70.9 1.1 copy-start.4
  72.0 48.2 %all-to-all-start.3 = ((bf16[4,3,32,2048]{3,2,1,0:T(8,128)(2,1)}), bf16[4,3,32,2048]{3,2,1,0:T(8,128)(2,1)}, u32[]{:S(2)}, u32[]{:S(2)}) async-start(bf16[4,3,32,2048]{3,2,1,0:T(8,128)(2,1)} %copy-done.4), calls=%async_computation.3 | async-start | bytes 3145728 | tf_op jit(solution)/shard_map/all_to_all | solution.py:271
  76.4 22.3 %collective-permute-start.1 = (bf16[16,128,384]{2,1,0:T(8,128)(2,1)}, bf16[16,128,384]{2,1,0:T(8,128)(2,1)S(1)}, u32[]{:S(2)}, u32[]{:S(2)}) collective-permute-start(bf16[16,128,384]{2,1,0:T(8,128)(2,1)} %copy-done.8), channel_id=1, source_target_pairs={{4,0},{8,4},{12,8},{5,1},{9,5},{13,9},{6,2},{10,6},{14,10},{7,3},{... | collective-permute-start | bytes 4718600 | tf_op jit(solution)/shard_map/ppermute | solution.py:268
  78.3 21.3 %collective-permute-start = (bf16[16,128,384]{2,1,0:T(8,128)(2,1)}, bf16[16,128,384]{2,1,0:T(8,128)(2,1)S(1)}, u32[]{:S(2)}, u32[]{:S(2)}) collective-permute-start(bf16[16,128,384]{2,1,0:T(8,128)(2,1)} %copy-done.8), channel_id=1, source_target_pairs={{0,4},{4,8},{8,12},{1,5},{5,9},{9,13},{2,6},{6,10},{10,14},{3,7},{... | collective-permute-start | bytes 4718600 | tf_op jit(solution)/shard_map/ppermute | solution.py:267
  99.6 1.4 copy-start.9
  119.1 1.1 copy-start.5
  120.3 35.3 %copy-start.11 = (f32[64,2048]{1,0:T(8,128)S(1)}, f32[64,2048]{1,0:T(8,128)}, u32[]{:S(2)}) copy-start(f32[64,2048]{1,0:T(8,128)} %refs_3_.1) | copy-start | bytes 1572868
  120.3 35.3 %copy-start.12 = (f32[3,2048]{1,0:T(4,128)S(1)}, f32[3,2048]{1,0:T(4,128)}, u32[]{:S(2)}) copy-start(f32[3,2048]{1,0:T(4,128)} %refs_4_.1) | copy-start | bytes 73732
  120.3 35.3 %all-to-all-start.1 = ((bf16[4,3,32,2048]{3,2,1,0:T(8,128)(2,1)}), bf16[4,3,32,2048]{3,2,1,0:T(8,128)(2,1)S(1)}, u32[]{:S(2)}, u32[]{:S(2)}) async-start(bf16[4,3,32,2048]{3,2,1,0:T(8,128)(2,1)} %copy-done.5), calls=%async_computation.1 | async-start | bytes 3145728 | tf_op jit(solution)/shard_map/all_to_all | solution.py:271
  155.6 2.8 %copy-start.2 = (f32[256,3,2048]{2,0,1:T(8,128)S(1)}, f32[256,3,2048]{2,0,1:T(8,128)}, u32[]{:S(2)}) copy-start(f32[256,3,2048]{2,0,1:T(8,128)} %param.10) | copy-start | bytes 18874372

commit v2 on v1

--- a/solution.py
+++ b/solution.py
@@ -7,9 +7,11 @@
 from jax.sharding import PartitionSpec as P
 
 CS = 128
-CHUNKS = 2
+CHUNKS = 1
+PIECES = 4
 GROUP = 8
 MIB = 1 << 20
+MESH = pl.DeviceIdType.MESH
 
 damping = 0.5
 speed_floor = 0.25
@@ -73,7 +75,7 @@
 
 def target_kernel(
     near_count, rank_width, src_ref, target_ref,
-    left_ref, own_ref, right_ref, block_ref, coef_ref, basis_ref,
+    mate_ref, own_ref, cross_ref, block_ref, coef_ref, basis_ref,
     out_ref, cells, acc, picked_c, picked_u, slot_list, slot_count, sems,
 ):
     t = pl.program_id(0)
@@ -85,7 +87,7 @@
     def _():
         copies = [
             pltpu.make_async_copy(ref, cells.at[pl.ds(i * clusters, clusters)], sems.at[i])
-            for i, ref in enumerate((left_ref, own_ref, right_ref))
+            for i, ref in enumerate((mate_ref, own_ref, cross_ref))
         ]
         for copy in copies:
             copy.start()
@@ -140,7 +142,7 @@
             out_ref[d, c] = acc[d * sub : (d + 1) * sub, c * CS : (c + 1) * CS].astype(jnp.bfloat16)
 
 
-def target_step(shares, src, target, left, own, right, blocks, coef, basis_u):
+def target_step(shares, src, target, mate, own, cross, blocks, coef, basis_u):
     clusters, members, width = own.shape
     near_count = blocks.shape[1]
     slots, rank_width, _ = coef.shape
@@ -178,7 +180,7 @@
             transcendentals=0,
         ),
         name="target",
-    )(src, target, left, own, right, blocks, coef, basis_u)
+    )(src, target, mate, own, cross, blocks, coef, basis_u)
 
 
 def law_kernel(chunks, col_ref, *refs):
@@ -223,6 +225,257 @@
         cost_estimate=pl.CostEstimate(flops=MIB * 16, bytes_accessed=8 * MIB, transcendentals=0),
         name="law",
     )(col, *parts, velocity, state, friction)
+
+
+def remote(src, dst, send, recv, axis, peer):
+    return pltpu.make_async_remote_copy(
+        src_ref=src,
+        dst_ref=dst,
+        send_sem=send,
+        recv_sem=recv,
+        device_id={axis: peer},
+        device_id_type=MESH,
+    )
+
+
+def exchange_kernel(
+    patches, cols, own, coef, mate_out, cross_out, arrived,
+    mate_sems, cross_send, cross_recv, share_send, share_recv, coef_send, coef_recv, local_sem,
+):
+    p = lax.axis_index("patch")
+    c = lax.axis_index("col")
+    odd = p % 2
+    mate = p + 1 - 2 * odd
+    cross = p + 2 * odd - 1
+    crosses = jnp.logical_and(cross >= 0, cross < patches)
+    per = own.shape[0] // cols
+    capacity = coef.shape[0] // patches
+
+    barrier = pltpu.get_barrier_semaphore()
+    for j in range(1, patches):
+        pl.semaphore_signal(barrier, inc=1, device_id={"patch": (p + j) % patches}, device_id_type=MESH)
+    for j in range(1, cols):
+        pl.semaphore_signal(barrier, inc=1, device_id={"col": (c + j) % cols}, device_id_type=MESH)
+    pl.semaphore_wait(barrier, patches + cols - 2)
+
+    def crossing(k):
+        at = c * per + k
+        return remote(own.at[at], cross_out.at[at], cross_send.at[k], cross_recv.at[k], "patch", cross)
+
+    def share(j, k):
+        at = c * per + k
+        return remote(
+            cross_out.at[at], cross_out.at[at], share_send.at[j - 1, k], share_recv.at[j - 1, k],
+            "col", (c + j) % cols,
+        )
+
+    def shared(j, k):
+        at = ((c + cols - j) % cols) * per + k
+        return remote(
+            cross_out.at[at], cross_out.at[at], share_send.at[j - 1, k], share_recv.at[j - 1, k],
+            "col", (c + j) % cols,
+        )
+
+    def coefficients(j):
+        q = (p + j) % patches
+        return remote(
+            coef.at[pl.ds(q * capacity, capacity)], arrived.at[pl.ds(p * capacity, capacity)],
+            coef_send.at[j - 1], coef_recv.at[j - 1], "patch", q,
+        )
+
+    def coefficients_in(j):
+        q = (p + patches - j) % patches
+        return remote(
+            coef.at[pl.ds(q * capacity, capacity)], arrived.at[pl.ds(q * capacity, capacity)],
+            coef_send.at[j - 1], coef_recv.at[j - 1], "patch", (p + j) % patches,
+        )
+
+    @pl.when(crosses)
+    def _():
+        for k in range(per):
+            crossing(k).start()
+
+    for j in range(1, patches):
+        coefficients(j).start()
+    to_mate = remote(own, mate_out, mate_sems.at[0], mate_sems.at[1], "patch", mate)
+    to_mate.start()
+    kept = pl.ds(p * capacity, capacity)
+    keep = pltpu.make_async_copy(coef.at[kept], arrived.at[kept], local_sem)
+    keep.start()
+
+    @pl.when(crosses)
+    def _():
+        for k in range(per):
+            crossing(k).wait_recv()
+            for j in range(1, cols):
+                share(j, k).start()
+        for k in range(per):
+            for j in range(1, cols):
+                shared(j, k).wait_recv()
+        for k in range(per):
+            crossing(k).wait_send()
+            for j in range(1, cols):
+                share(j, k).wait_send()
+
+    keep.wait()
+    to_mate.wait()
+    for j in range(1, patches):
+        coefficients_in(j).wait_recv()
+        coefficients(j).wait_send()
+
+
+def exchange_step(patches, cols, own, coef):
+    per = own.shape[0] // cols
+    dma = pltpu.SemaphoreType.DMA
+    return pl.pallas_call(
+        functools.partial(exchange_kernel, patches, cols),
+        in_specs=[pl.BlockSpec(memory_space=pl.ANY)] * 2,
+        out_specs=[pl.BlockSpec(memory_space=pl.ANY)] * 3,
+        out_shape=[
+            jax.ShapeDtypeStruct(own.shape, own.dtype),
+            jax.ShapeDtypeStruct(own.shape, own.dtype),
+            jax.ShapeDtypeStruct(coef.shape, coef.dtype),
+        ],
+        scratch_shapes=[
+            dma((2,)),
+            dma((per,)),
+            dma((per,)),
+            dma((cols - 1, per)),
+            dma((cols - 1, per)),
+            dma((patches - 1,)),
+            dma((patches - 1,)),
+            dma(()),
+        ],
+        compiler_params=pltpu.CompilerParams(
+            collective_id=0, has_side_effects=True, vmem_limit_bytes=8 * MIB
+        ),
+        name="exchange",
+    )(own, coef)
+
+
+def line_kernel(
+    cols, part_ref, out_ref, up_in, up_out, down_in, down_out,
+    up_send, up_recv, down_send, down_recv,
+):
+    me = lax.axis_index("col")
+    width = part_ref.shape[3] // PIECES
+    not_first = me > 0
+    not_last = me < cols - 1
+
+    barrier = pltpu.get_barrier_semaphore()
+
+    @pl.when(not_first)
+    def _():
+        pl.semaphore_signal(barrier, inc=1, device_id={"col": me - 1}, device_id_type=MESH)
+
+    @pl.when(not_last)
+    def _():
+        pl.semaphore_signal(barrier, inc=1, device_id={"col": me + 1}, device_id_type=MESH)
+
+    pl.semaphore_wait(barrier, jnp.where(jnp.logical_and(not_first, not_last), 2, 1))
+
+    def span(k):
+        return pl.ds(pl.multiple_of(k * width, width), width)
+
+    def hop(up, d, k):
+        out, into = (up_out, up_in) if up else (down_out, down_in)
+        send, recv = (up_send, up_recv) if up else (down_send, down_recv)
+        peer = me + 1 if up else me - 1
+        piece = (d, slice(None), slice(None), span(k))
+        return remote(out.at[piece], into.at[piece], send.at[d, k], recv.at[d, k], "col", peer)
+
+    def step(up, d, k):
+        out, into = (up_out, up_in) if up else (down_out, down_in)
+        more = not_first if up else not_last
+        piece = (d, slice(None), slice(None), span(k))
+
+        @pl.when(more)
+        def _():
+            hop(up, d, k).wait_recv()
+            total = part_ref[piece].astype(jnp.float32) + into[piece].astype(jnp.float32)
+            out[piece] = total.astype(jnp.bfloat16)
+
+        @pl.when(jnp.logical_not(more))
+        def _():
+            out[piece] = part_ref[piece]
+
+        hop(up, d, k).start()
+
+    count = (cols - 1) * PIECES
+    up_first = me < cols - 1 - me
+
+    def send_all(i, carry):
+        j, k = i // PIECES, i % PIECES
+        high, low = cols - 1 - j, j
+        sends_up = high > me
+        sends_down = low < me
+
+        @pl.when(jnp.logical_and(sends_up, up_first))
+        def _():
+            step(True, high, k)
+
+        @pl.when(sends_down)
+        def _():
+            step(False, low, k)
+
+        @pl.when(jnp.logical_and(sends_up, jnp.logical_not(up_first)))
+        def _():
+            step(True, high, k)
+
+        return carry
+
+    lax.fori_loop(0, count, send_all, 0)
+
+    def finish(k, carry):
+        piece = (me, slice(None), slice(None), span(k))
+        goal = (slice(None), slice(None), span(k))
+        out_ref[goal] = part_ref[piece].astype(jnp.float32)
+
+        @pl.when(not_first)
+        def _():
+            hop(True, me, k).wait_recv()
+            out_ref[goal] += up_in[piece].astype(jnp.float32)
+
+        @pl.when(not_last)
+        def _():
+            hop(False, me, k).wait_recv()
+            out_ref[goal] += down_in[piece].astype(jnp.float32)
+
+        return carry
+
+    lax.fori_loop(0, PIECES, finish, 0)
+
+    def settle(i, carry):
+        j, k = i // PIECES, i % PIECES
+        high, low = cols - 1 - j, j
+
+        @pl.when(high > me)
+        def _():
+            hop(True, high, k).wait_send()
+
+        @pl.when(low < me)
+        def _():
+            hop(False, low, k).wait_send()
+
+        return carry
+
+    lax.fori_loop(0, count, settle, 0)
+
+
+def line_step(partial):
+    cols, _, sub, row_cells = partial.shape
+    dma = pltpu.SemaphoreType.DMA
+    return pl.pallas_call(
+        functools.partial(line_kernel, cols),
+        in_specs=[pl.BlockSpec(memory_space=pltpu.VMEM)],
+        out_specs=pl.BlockSpec(memory_space=pltpu.VMEM),
+        out_shape=jax.ShapeDtypeStruct((3, sub, row_cells), jnp.float32),
+        scratch_shapes=[pltpu.VMEM(partial.shape, jnp.bfloat16)] * 4 + [dma((cols, PIECES))] * 4,
+        compiler_params=pltpu.CompilerParams(
+            collective_id=1, has_side_effects=True, vmem_limit_bytes=32 * MIB
+        ),
+        name="line",
+    )(partial)
 
 
 def shards(
@@ -256,19 +509,15 @@
     dest = far_dest.reshape(-1)
     rank = far_rank.reshape(-1)
     target = far_target.reshape(-1)
-    first = lax.axis_index("patch") * clusters - clusters
-    src = (near_src - first).reshape(-1)
-    ends = patches - 1
-    up = [(i, i + 1) for i in range(ends)]
-    down = [(i + 1, i) for i in range(ends)]
-    parts = []
-    for h in range(CHUNKS):
-        own, coef = source_step(h, split, basis_v, dest, rank)(slots)
-        left = lax.ppermute(own, "patch", up)
-        right = lax.ppermute(own, "patch", down)
-        arrived = lax.all_to_all(coef, "patch", split_axis=0, concat_axis=0, tiled=True)
-        partial = target_step(shares, src, target, left, own, right, blocks, arrived, basis_u)
-        parts.append(lax.all_to_all(partial, "col", split_axis=0, concat_axis=0, tiled=True))
+    at_patch = lax.axis_index("patch")
+    offset = near_src - (at_patch - 1) * clusters
+    row, cell = offset // clusters, offset % clusters
+    row = jnp.where(at_patch % 2 == 0, 2 - row, row)
+    src = (row * clusters + cell).reshape(-1)
+    own, coef = source_step(0, split, basis_v, dest, rank)(slots)
+    mate, cross, arrived = exchange_step(patches, shares, own, coef)
+    partial = target_step(shares, src, target, mate, own, cross, blocks, arrived, basis_u)
+    parts = [line_step(partial)[None]]
     col = lax.axis_index("col").reshape(1).astype(jnp.int32)
     rate = law_step(col, parts, planes, state, friction)
     return jnp.transpose(rate, (1, 0, 2))

time: 164 us -> 124 us (0.76)
  the two profiles are of different devices: /device:TPU:1 before, /device:TPU:10 now
where the time goes in v2:
time: 124 us
  Pallas kernels  116 us (94%)
  local copies, waits for them, and re-layouts  6.85 us (6%)
    pallas_call x1, Pallas kernels, line_step(): pl.pallas_call(functools.partial(line_kernel, cols), in_specs=[pl.BlockSp...  45.5 us
    pallas_call x1, Pallas kernels, exchange_step(): pl.pallas_call(functools.partial(exchange_kernel, patches, cols), in_spec...  44 us
    pallas_call x1, Pallas kernels, target_step(): pl.pallas_call(functools.partial(target_kernel, near_count, rank_width),...  19.2 us
    unnamed x16, local copies, waits for them, and re-layouts  5.74 us
    pallas_call x1, Pallas kernels, call(): pl.pallas_call(functools.partial(source_kernel, far_count, rank_width), g...  5.33 us

profile of v2, /device:TPU:10, one launch (start us, length us, event | category | flops | bytes accessed | tf_op | source)
XLA Modules:
  0.0 123.9 jit_solution(17904152393086487821)
XLA Ops:
  0.0 0.7 fusion.1
  0.7 0.8 reshape.26.target_ref
  1.5 0.1 copy.15
  1.5 0.1 reshape.25.src_ref
  1.6 0.8 copy.16
  2.4 0.1 reshape.27.dest_ref
  2.5 0.8 copy.17
  3.2 0.1 reshape.28.rank_ref
  3.3 0.0 copy-start
  3.3 2.8 %copy-done = f32[256,3,2048]{2,0,1:T(8,128)S(1)} copy-done((f32[256,3,2048]{2,0,1:T(8,128)S(1)}, f32[256,3,2048]{2,0,1:T(8,128)}, u32[]{:S(2)}) %copy-start) | copy-done | bytes 6291480
  6.1 0.0 copy-start.2
  6.1 1.4 %copy-done.2 = bf16[1,16,4,32,384]{4,3,2,1,0:T(8,128)(2,1)S(1)} copy-done((bf16[1,16,4,32,384]{4,3,2,1,0:T(8,128)(2,1)S(1)}, bf16[1,16,4,32,384]{4,3,2,1,0:T(8,128)(2,1)}, u32[]{:S(2)}) %copy-start.2) | copy-done | bytes 1572888
  7.5 5.3 %source.1 = (bf16[16,256,384]{2,1,0:T(8,128)(2,1)S(1)}, bf16[128,32,256]{2,1,0:T(8,128)(2,1)S(1)}) custom-call(s32[64]{0:T(128)S(1)} %reshape.27.dest_ref, s32[64]{0:T(128)S(1)} %reshape.28.rank_ref, f32[3,4,1,64,2048]{4,3,2,1,0:T(8,128)S(1)} %bitcast.10, bf16[16,128,384]{2,1,0:T(8,128)(2,1)S(1)} %bitcast.16), custom_call_target="tpu_custom_call" | custom-call | flops 402653184 | bytes 8388608 | tf_op jit(solution)/shard_map/source/pallas_call | solution.py:46
  12.9 0.0 copy-start.1
  12.9 44.0 %exchange.1 = (bf16[16,256,384]{2,1,0:T(8,128)(2,1)S(1)}, bf16[16,256,384]{2,1,0:T(8,128)(2,1)S(1)}, bf16[128,32,256]{2,1,0:T(8,128)(2,1)S(1)}) custom-call(bf16[16,256,384]{2,1,0:T(8,128)(2,1)S(1)} %get-tuple-element.10.own.own_ref, bf16[128,32,256]{2,1,0:T(8,128)(2,1)S(1)} %get-tuple-element.11.coef), custom_call_target="tpu_custom_call" | custom-call | tf_op jit(solution)/shard_map/exchange/pallas_call | solution.py:330
  56.9 0.0 slice-start
  56.9 0.0 copy-done.1
  56.9 0.0 slice-start.1
  56.9 19.2 %target.1.part_ref = bf16[4,3,64,2048]{3,2,1,0:T(8,128)(2,1)S(1)} custom-call(s32[32]{0:T(128)S(1)} %reshape.25.src_ref, s32[128]{0:T(128)S(1)} %reshape.26.target_ref, bf16[16,256,384]{2,1,0:T(8,128)(2,1)S(1)} %get-tuple-element.12.mate_ref, bf16[16,256,384]{2,1,0:T(8,128)(2,1)S(1)} %get-tuple-element.10.own.own_ref, ...), custom_call_target="tpu_custom_call" | custom-call | flops 3221225472 | bytes 25165824 | tf_op jit(solution)/shard_map/target/pallas_call | solution.py:151
  76.1 0.0 copy-start.3
  76.1 0.0 copy-start.4
  76.2 45.5 %line.1 = f32[3,64,2048]{2,1,0:T(8,128)S(1)} custom-call(bf16[4,3,64,2048]{3,2,1,0:T(8,128)(2,1)S(1)} %target.1.part_ref), custom_call_target="tpu_custom_call" | custom-call | tf_op jit(solution)/shard_map/line/pallas_call | solution.py:468
  121.6 0.0 slice-done
  121.7 0.0 slice-done.1
  121.7 0.0 copy-done.3
  121.7 0.0 copy-done.4
  121.7 2.2 %law.1 = f32[3,64,2048]{2,1,0:T(8,128)} custom-call(s32[1]{0:T(128)} %bitcast.col_ref, f32[1,3,64,2048]{3,2,1,0:T(8,128)S(1)} %bitcast.14, f32[3,256,2048]{2,1,0:T(8,128)S(1)} %bitcast.13, f32[64,2048]{1,0:T(8,128)S(1)} %copy-done.3, f32[3,2048]{1,0:T(4,128)S(1)} %copy-done.4), custom_call_target="tpu_custom_call" | custom-call | flops 16777216 | bytes 8388608 | tf_op jit(solution)/shard_map/law/pallas_call | solution.py:210
  (1 shorter events, 0.0 us)
Async XLA Ops:
  3.3 2.8 %copy-start = (f32[256,3,2048]{2,0,1:T(8,128)S(1)}, f32[256,3,2048]{2,0,1:T(8,128)}, u32[]{:S(2)}) copy-start(f32[256,3,2048]{2,0,1:T(8,128)} %param.10) | copy-start | bytes 18874372
  6.1 1.4 %copy-start.2 = (bf16[1,16,4,32,384]{4,3,2,1,0:T(8,128)(2,1)S(1)}, bf16[1,16,4,32,384]{4,3,2,1,0:T(8,128)(2,1)}, u32[]{:S(2)}) copy-start(bf16[1,16,4,32,384]{4,3,2,1,0:T(8,128)(2,1)} %param.17) | copy-start | bytes 4718596
  12.9 44.0 %copy-start.1 = (bf16[1,1,4,32,32,384]{5,4,3,2,1,0:T(8,128)(2,1)S(1)}, bf16[1,1,4,32,32,384]{5,4,3,2,1,0:T(8,128)(2,1)}, u32[]{:S(2)}) copy-start(bf16[1,1,4,32,32,384]{5,4,3,2,1,0:T(8,128)(2,1)} %param.19) | copy-start | bytes 9437188
  56.9 64.8 %slice-start = ((s8[6291456]{0:T(1024)(128)(4,1)}), s8[4194304]{0:T(1024)(128)(4,1)S(1)}, s32[]{:S(2)}) async-start(s8[6291456]{0:T(1024)(128)(4,1)} %bitcast.11), calls=%async_computation | async-start | bytes 8388608
  56.9 64.8 %slice-start.1 = ((s8[6291456]{0:T(1024)(128)(4,1)}), s8[2097152]{0:T(1024)(128)(4,1)S(1)}, s32[]{:S(2)}) async-start(s8[6291456]{0:T(1024)(128)(4,1)} %bitcast.11), calls=%async_computation.1 | async-start | bytes 4194304
  76.1 45.5 %copy-start.3 = (f32[64,2048]{1,0:T(8,128)S(1)}, f32[64,2048]{1,0:T(8,128)}, u32[]{:S(2)}) copy-start(f32[64,2048]{1,0:T(8,128)} %refs_2_.1) | copy-start | bytes 1572868
  76.1 45.5 %copy-start.4 = (f32[3,2048]{1,0:T(4,128)S(1)}, f32[3,2048]{1,0:T(4,128)}, u32[]{:S(2)}) copy-start(f32[3,2048]{1,0:T(4,128)} %refs_3_.1) | copy-start | bytes 73732

commit v3 on v2

--- a/solution.py
+++ b/solution.py
@@ -75,23 +75,16 @@
 
 def target_kernel(
     near_count, rank_width, src_ref, target_ref,
-    mate_ref, own_ref, cross_ref, block_ref, coef_ref, basis_ref,
-    out_ref, cells, acc, picked_c, picked_u, slot_list, slot_count, sems,
+    cells, block_ref, coef_ref, basis_ref,
+    out_ref, acc, picked_c, picked_u, slot_list, slot_count,
 ):
     t = pl.program_id(0)
-    clusters = own_ref.shape[0]
+    clusters = cells.shape[0] // 3
     slots = coef_ref.shape[0]
     shares, _, sub, _ = out_ref.shape
 
     @pl.when(t == 0)
     def _():
-        copies = [
-            pltpu.make_async_copy(ref, cells.at[pl.ds(i * clusters, clusters)], sems.at[i])
-            for i, ref in enumerate((mate_ref, own_ref, cross_ref))
-        ]
-        for copy in copies:
-            copy.start()
-
         def clear(i, carry):
             slot_count[i] = 0
             return carry
@@ -110,8 +103,6 @@
             return carry
 
         lax.fori_loop(0, slots, place, 0)
-        for copy in copies:
-            copy.wait()
 
     total = None
     for j in range(near_count):
@@ -142,45 +133,41 @@
             out_ref[d, c] = acc[d * sub : (d + 1) * sub, c * CS : (c + 1) * CS].astype(jnp.bfloat16)
 
 
-def target_step(shares, src, target, mate, own, cross, blocks, coef, basis_u):
-    clusters, members, width = own.shape
+def target_step(shares, src, target, cells, blocks, coef, basis_u):
+    clusters = cells.shape[0] // 3
+    _, members, width = cells.shape
     near_count = blocks.shape[1]
     slots, rank_width, _ = coef.shape
     sub = members // shares
-    whole = lambda t, *_: (0, 0, 0)
     return pl.pallas_call(
         functools.partial(target_kernel, near_count, rank_width),
         grid_spec=pltpu.PrefetchScalarGridSpec(
             num_scalar_prefetch=2,
             grid=(clusters,),
             in_specs=[
-                pl.BlockSpec(memory_space=pl.ANY),
-                pl.BlockSpec(memory_space=pl.ANY),
-                pl.BlockSpec(memory_space=pl.ANY),
+                pl.BlockSpec(memory_space=pltpu.VMEM),
                 pl.BlockSpec((1, near_count, width, width), lambda t, *_: (t, 0, 0, 0)),
-                pl.BlockSpec((slots, rank_width, members), whole),
-                pl.BlockSpec((slots, rank_width, width), whole),
+                pl.BlockSpec(memory_space=pltpu.VMEM),
+                pl.BlockSpec(memory_space=pltpu.VMEM),
             ],
             out_specs=pl.BlockSpec((shares, 3, sub, CS), lambda t, *_: (0, 0, 0, t)),
             scratch_shapes=[
-                pltpu.VMEM((3 * clusters, members, width), jnp.bfloat16),
                 pltpu.VMEM((members, width), jnp.float32),
                 pltpu.VMEM((GROUP * rank_width, members), jnp.bfloat16),
                 pltpu.VMEM((GROUP * rank_width, width), jnp.bfloat16),
                 pltpu.SMEM((clusters * slots,), jnp.int32),
                 pltpu.SMEM((clusters,), jnp.int32),
-                pltpu.SemaphoreType.DMA((3,)),
             ],
         ),
         out_shape=jax.ShapeDtypeStruct((shares, 3, sub, clusters * CS), jnp.bfloat16),
-        compiler_params=pltpu.CompilerParams(vmem_limit_bytes=36 * MIB),
+        compiler_params=pltpu.CompilerParams(vmem_limit_bytes=34 * MIB),
         cost_estimate=pl.CostEstimate(
             flops=2 * clusters * members * width * (near_count * width + GROUP * rank_width),
             bytes_accessed=24 * MIB,
             transcendentals=0,
         ),
         name="target",
-    )(src, target, mate, own, cross, blocks, coef, basis_u)
+    )(src, target, cells, blocks, coef, basis_u)
 
 
 def law_kernel(chunks, col_ref, *refs):
@@ -239,8 +226,8 @@
 
 
 def exchange_kernel(
-    patches, cols, own, coef, mate_out, cross_out, arrived,
-    mate_sems, cross_send, cross_recv, share_send, share_recv, coef_send, coef_recv, local_sem,
+    patches, cols, own, coef, cells, arrived,
+    mate_sems, cross_send, cross_recv, share_send, share_recv, coef_send, coef_recv, local_sems,
 ):
     p = lax.axis_index("patch")
     c = lax.axis_index("col")
@@ -251,6 +238,11 @@
     per = own.shape[0] // cols
     capacity = coef.shape[0] // patches
 
+    clusters = own.shape[0]
+    mate_out = cells.at[pl.ds(0, clusters)]
+    own_out = cells.at[pl.ds(clusters, clusters)]
+    cross_at = 2 * clusters
+    place = pltpu.make_async_copy(own, own_out, local_sems.at[1])
     barrier = pltpu.get_barrier_semaphore()
     for j in range(1, patches):
         pl.semaphore_signal(barrier, inc=1, device_id={"patch": (p + j) % patches}, device_id_type=MESH)
@@ -260,19 +252,19 @@
 
     def crossing(k):
         at = c * per + k
-        return remote(own.at[at], cross_out.at[at], cross_send.at[k], cross_recv.at[k], "patch", cross)
+        return remote(own.at[at], cells.at[cross_at + at], cross_send.at[k], cross_recv.at[k], "patch", cross)
 
     def share(j, k):
         at = c * per + k
         return remote(
-            cross_out.at[at], cross_out.at[at], share_send.at[j - 1, k], share_recv.at[j - 1, k],
+            cells.at[cross_at + at], cells.at[cross_at + at], share_send.at[j - 1, k], share_recv.at[j - 1, k],
             "col", (c + j) % cols,
         )
 
     def shared(j, k):
         at = ((c + cols - j) % cols) * per + k
         return remote(
-            cross_out.at[at], cross_out.at[at], share_send.at[j - 1, k], share_recv.at[j - 1, k],
+            cells.at[cross_at + at], cells.at[cross_at + at], share_send.at[j - 1, k], share_recv.at[j - 1, k],
             "col", (c + j) % cols,
         )
 
@@ -290,18 +282,18 @@
             coef_send.at[j - 1], coef_recv.at[j - 1], "patch", (p + j) % patches,
         )
 
+    to_mate = remote(own, mate_out, mate_sems.at[0], mate_sems.at[1], "patch", mate)
+    kept = pl.ds(p * capacity, capacity)
+    keep = pltpu.make_async_copy(coef.at[kept], arrived.at[kept], local_sems.at[0])
+
     @pl.when(crosses)
     def _():
         for k in range(per):
             crossing(k).start()
 
-    for j in range(1, patches):
-        coefficients(j).start()
-    to_mate = remote(own, mate_out, mate_sems.at[0], mate_sems.at[1], "patch", mate)
     to_mate.start()
-    kept = pl.ds(p * capacity, capacity)
-    keep = pltpu.make_async_copy(coef.at[kept], arrived.at[kept], local_sem)
     keep.start()
+    place.start()
 
     @pl.when(crosses)
     def _():
@@ -309,6 +301,13 @@
             crossing(k).wait_recv()
             for j in range(1, cols):
                 share(j, k).start()
+
+    to_mate.wait_recv()
+    for j in range(1, patches):
+        coefficients(j).start()
+
+    @pl.when(crosses)
+    def _():
         for k in range(per):
             for j in range(1, cols):
                 shared(j, k).wait_recv()
@@ -318,7 +317,8 @@
                 share(j, k).wait_send()
 
     keep.wait()
-    to_mate.wait()
+    place.wait()
+    to_mate.wait_send()
     for j in range(1, patches):
         coefficients_in(j).wait_recv()
         coefficients(j).wait_send()
@@ -329,11 +329,10 @@
     dma = pltpu.SemaphoreType.DMA
     return pl.pallas_call(
         functools.partial(exchange_kernel, patches, cols),
-        in_specs=[pl.BlockSpec(memory_space=pl.ANY)] * 2,
-        out_specs=[pl.BlockSpec(memory_space=pl.ANY)] * 3,
+        in_specs=[pl.BlockSpec(memory_space=pltpu.VMEM)] * 2,
+        out_specs=[pl.BlockSpec(memory_space=pltpu.VMEM)] * 2,
         out_shape=[
-            jax.ShapeDtypeStruct(own.shape, own.dtype),
-            jax.ShapeDtypeStruct(own.shape, own.dtype),
+            jax.ShapeDtypeStruct((3 * own.shape[0],) + own.shape[1:], own.dtype),
             jax.ShapeDtypeStruct(coef.shape, coef.dtype),
         ],
         scratch_shapes=[
@@ -344,7 +343,7 @@
             dma((cols - 1, per)),
             dma((patches - 1,)),
             dma((patches - 1,)),
-            dma(()),
+            dma((2,)),
         ],
         compiler_params=pltpu.CompilerParams(
             collective_id=0, has_side_effects=True, vmem_limit_bytes=8 * MIB
@@ -515,8 +514,8 @@
     row = jnp.where(at_patch % 2 == 0, 2 - row, row)
     src = (row * clusters + cell).reshape(-1)
     own, coef = source_step(0, split, basis_v, dest, rank)(slots)
-    mate, cross, arrived = exchange_step(patches, shares, own, coef)
-    partial = target_step(shares, src, target, mate, own, cross, blocks, arrived, basis_u)
+    cells, arrived = exchange_step(patches, shares, own, coef)
+    partial = target_step(shares, src, target, cells, blocks, arrived, basis_u)
     parts = [line_step(partial)[None]]
     col = lax.axis_index("col").reshape(1).astype(jnp.int32)
     rate = law_step(col, parts, planes, state, friction)

time: 124 us -> 135 us (1.089)
  local copies, waits for them, and re-layouts: 6.85 us -> 19.2 us
  Pallas kernels: 116 us -> 114 us
    unnamed x16 -> x24, local copies, waits for them, and re-layouts: 5.74 us -> 18.8 us
    pallas_call x1, Pallas kernels: 44 us -> 42.6 us  [exchange_step(): pl.pallas_call(functools.partial(exchange_kernel, patches, cols), in_spec...]
    pallas_call x1, Pallas kernels: 19.2 us -> 17.8 us  [target_step(): pl.pallas_call(functools.partial(target_kernel, near_count, rank_width),...]
where the time goes in v3:
time: 135 us; the launch traced here: 134 us
  Pallas kernels  114 us (84%)
  local copies, waits for them, and re-layouts  19.2 us (14%)
    pallas_call x1, Pallas kernels, line_step(): pl.pallas_call(functools.partial(line_kernel, cols), in_specs=[pl.BlockSp...  45.7 us
    pallas_call x1, Pallas kernels, exchange_step(): pl.pallas_call(functools.partial(exchange_kernel, patches, cols), in_spec...  42.6 us
    unnamed x24, local copies, waits for them, and re-layouts  18.8 us
    pallas_call x1, Pallas kernels, target_step(): pl.pallas_call(functools.partial(target_kernel, near_count, rank_width),...  17.8 us
    pallas_call x1, Pallas kernels, call(): pl.pallas_call(functools.partial(source_kernel, far_count, rank_width), g...  5.33 us

profile of v3, /device:TPU:10, one launch (start us, length us, event | category | flops | bytes accessed | tf_op | source)
XLA Modules:
  0.0 133.6 jit_solution(5705099871530641058)
XLA Ops:
  0.0 0.7 fusion.1
  0.7 0.1 copy.15
  0.8 0.1 reshape.25.src_ref
  0.9 0.8 copy.16
  1.6 0.1 reshape.27.dest_ref
  1.7 0.8 copy.17
  2.5 0.1 reshape.28.rank_ref
  2.6 0.0 copy-start
  2.6 2.8 %copy-done = f32[256,3,2048]{2,0,1:T(8,128)S(1)} copy-done((f32[256,3,2048]{2,0,1:T(8,128)S(1)}, f32[256,3,2048]{2,0,1:T(8,128)}, u32[]{:S(2)}) %copy-start) | copy-done | bytes 6291480
  5.4 0.0 copy-start.7
  5.4 1.4 %copy-done.7 = bf16[1,16,4,32,384]{4,3,2,1,0:T(8,128)(2,1)S(1)} copy-done((bf16[1,16,4,32,384]{4,3,2,1,0:T(8,128)(2,1)S(1)}, bf16[1,16,4,32,384]{4,3,2,1,0:T(8,128)(2,1)}, u32[]{:S(2)}) %copy-start.7) | copy-done | bytes 1572888
  6.8 5.3 %source.1 = (bf16[16,256,384]{2,1,0:T(8,128)(2,1)S(1)}, bf16[128,32,256]{2,1,0:T(8,128)(2,1)S(1)}) custom-call(s32[64]{0:T(128)S(1)} %reshape.27.dest_ref, s32[64]{0:T(128)S(1)} %reshape.28.rank_ref, f32[3,4,1,64,2048]{4,3,2,1,0:T(8,128)S(1)} %bitcast.10, bf16[16,128,384]{2,1,0:T(8,128)(2,1)S(1)} %bitcast.14), custom_call_target="tpu_custom_call" | custom-call | flops 402653184 | bytes 8388608 | tf_op jit(solution)/shard_map/source/pallas_call | solution.py:46
  12.1 0.0 copy-start.10
  12.1 0.0 copy-start.4
  12.1 42.6 %exchange.1 = (bf16[48,256,384]{2,1,0:T(8,128)(2,1)S(1)}, bf16[128,32,256]{2,1,0:T(8,128)(2,1)S(1)}) custom-call(bf16[16,256,384]{2,1,0:T(8,128)(2,1)S(1)} %get-tuple-element.9.own, bf16[128,32,256]{2,1,0:T(8,128)(2,1)S(1)} %get-tuple-element.10.coef), custom_call_target="tpu_custom_call" | custom-call | tf_op jit(solution)/shard_map/exchange/pallas_call | solution.py:330
  54.7 0.0 copy-start.2
  54.7 3.6 %copy-done.2 = bf16[48,256,384]{2,1,0:T(8,128)(2,1)} copy-done((bf16[48,256,384]{2,1,0:T(8,128)(2,1)}, bf16[48,256,384]{2,1,0:T(8,128)(2,1)S(1)}, u32[]{:S(2)}) %copy-start.2) | copy-done | bytes 9437208
  58.3 1.3 copy-done.5
  59.7 0.0 copy-done.10
  59.7 0.1 reshape.26.target_ref
  59.7 0.0 copy-done.4
  59.7 3.7 %copy-done.3 = bf16[48,256,384]{2,1,0:T(8,128)(2,1)S(1)} copy-done((bf16[48,256,384]{2,1,0:T(8,128)(2,1)S(1)}, bf16[48,256,384]{2,1,0:T(8,128)(2,1)}, u32[]{:S(2)}) %copy-start.3) | copy-done | bytes 9437208
  63.4 1.6 %copy-done.6 = bf16[128,32,256]{2,1,0:T(8,128)(2,1)S(1)} copy-done((bf16[128,32,256]{2,1,0:T(8,128)(2,1)S(1)}, bf16[128,32,256]{2,1,0:T(8,128)(2,1)}, u32[]{:S(2)}) %copy-start.6) | copy-done | bytes 2097176
  65.0 17.8 %target.1.part_ref = bf16[4,3,64,2048]{3,2,1,0:T(8,128)(2,1)S(1)} custom-call(s32[32]{0:T(128)S(1)} %reshape.25.src_ref, s32[128]{0:T(128)S(1)} %reshape.26.target_ref, bf16[48,256,384]{2,1,0:T(8,128)(2,1)S(1)} %copy-done.3, bf16[16,2,384,384]{3,2,1,0:T(8,128)(2,1)} %block_ref.1, bf16[128,32,256]{2,1,0:T(8,128)(2,1)S(1)} %copy-done.6, ...), custom_call_target="tpu_custom_call" | custom-call | flops 3221225472 | bytes 25165824 | tf_op jit(solution)/shard_map/target/pallas_call | solution.py:142
  82.8 0.0 copy-start.8
  82.8 0.0 copy-start.9
  82.8 45.7 %line.1 = f32[3,64,2048]{2,1,0:T(8,128)S(1)} custom-call(bf16[4,3,64,2048]{3,2,1,0:T(8,128)(2,1)S(1)} %target.1.part_ref), custom_call_target="tpu_custom_call" | custom-call | tf_op jit(solution)/shard_map/line/pallas_call | solution.py:467
  128.6 0.0 copy-done.8
  128.6 0.0 copy-done.9
  128.6 0.0 copy-start.1
  128.6 2.8 %copy-done.1 = f32[256,3,2048]{2,0,1:T(8,128)S(1)} copy-done((f32[256,3,2048]{2,0,1:T(8,128)S(1)}, f32[256,3,2048]{2,0,1:T(8,128)}, u32[]{:S(2)}) %copy-start.1) | copy-done | bytes 6291480
  131.4 2.2 %law.1 = f32[3,64,2048]{2,1,0:T(8,128)} custom-call(s32[1]{0:T(128)} %bitcast.col_ref, f32[1,3,64,2048]{3,2,1,0:T(8,128)S(1)} %bitcast.12, f32[3,256,2048]{2,1,0:T(8,128)S(1)} %bitcast.11, f32[64,2048]{1,0:T(8,128)S(1)} %copy-done.8, f32[3,2048]{1,0:T(4,128)S(1)} %copy-done.9), custom_call_target="tpu_custom_call" | custom-call | flops 16777216 | bytes 8388608 | tf_op jit(solution)/shard_map/law/pallas_call | solution.py:197
  (3 shorter events, 0.0 us)
Async XLA Ops:
  2.6 2.8 %copy-start = (f32[256,3,2048]{2,0,1:T(8,128)S(1)}, f32[256,3,2048]{2,0,1:T(8,128)}, u32[]{:S(2)}) copy-start(f32[256,3,2048]{2,0,1:T(8,128)} %param.10) | copy-start | bytes 18874372
  5.4 1.4 %copy-start.7 = (bf16[1,16,4,32,384]{4,3,2,1,0:T(8,128)(2,1)S(1)}, bf16[1,16,4,32,384]{4,3,2,1,0:T(8,128)(2,1)}, u32[]{:S(2)}) copy-start(bf16[1,16,4,32,384]{4,3,2,1,0:T(8,128)(2,1)} %param.17) | copy-start | bytes 4718596
  12.1 47.6 %copy-start.10 = (s32[1,1,4,32]{3,2,1,0:T(4,128)S(1)}, s32[1,1,4,32]{3,2,1,0:T(4,128)}, u32[]{:S(2)}) copy-start(s32[1,1,4,32]{3,2,1,0:T(4,128)} %param.18) | copy-start | bytes 1540
  12.1 47.6 %copy-start.4 = (bf16[1,1,4,32,32,384]{5,4,3,2,1,0:T(8,128)(2,1)S(1)}, bf16[1,1,4,32,32,384]{5,4,3,2,1,0:T(8,128)(2,1)}, u32[]{:S(2)}) copy-start(bf16[1,1,4,32,32,384]{5,4,3,2,1,0:T(8,128)(2,1)} %param.19) | copy-start | bytes 9437188
  54.7 3.7 %copy-start.2 = (bf16[48,256,384]{2,1,0:T(8,128)(2,1)}, bf16[48,256,384]{2,1,0:T(8,128)(2,1)S(1)}, u32[]{:S(2)}) copy-start(bf16[48,256,384]{2,1,0:T(8,128)(2,1)S(1)} %get-tuple-element.11.cells) | copy-start | bytes 28311556
  58.3 1.3 copy-start.5
  59.7 3.7 %copy-start.3 = (bf16[48,256,384]{2,1,0:T(8,128)(2,1)S(1)}, bf16[48,256,384]{2,1,0:T(8,128)(2,1)}, u32[]{:S(2)}) copy-start(bf16[48,256,384]{2,1,0:T(8,128)(2,1)} %copy-done.2) | copy-start | bytes 28311556
  63.4 1.6 %copy-start.6 = (bf16[128,32,256]{2,1,0:T(8,128)(2,1)S(1)}, bf16[128,32,256]{2,1,0:T(8,128)(2,1)}, u32[]{:S(2)}) copy-start(bf16[128,32,256]{2,1,0:T(8,128)(2,1)} %copy-done.5) | copy-start | bytes 6291460
  82.8 45.8 %copy-start.8 = (f32[64,2048]{1,0:T(8,128)S(1)}, f32[64,2048]{1,0:T(8,128)}, u32[]{:S(2)}) copy-start(f32[64,2048]{1,0:T(8,128)} %refs_2_.1) | copy-start | bytes 1572868
  82.8 45.8 %copy-start.9 = (f32[3,2048]{1,0:T(4,128)S(1)}, f32[3,2048]{1,0:T(4,128)}, u32[]{:S(2)}) copy-start(f32[3,2048]{1,0:T(4,128)} %refs_3_.1) | copy-start | bytes 73732
  128.6 2.8 %copy-start.1 = (f32[256,3,2048]{2,0,1:T(8,128)S(1)}, f32[256,3,2048]{2,0,1:T(8,128)}, u32[]{:S(2)}) copy-start(f32[256,3,2048]{2,0,1:T(8,128)} %param.10) | copy-start | bytes 18874372

commit v4 on v2

--- a/solution.py
+++ b/solution.py
@@ -8,7 +8,7 @@
 
 CS = 128
 CHUNKS = 1
-PIECES = 4
+PIECES = 8
 GROUP = 8
 MIB = 1 << 20
 MESH = pl.DeviceIdType.MESH
@@ -240,7 +240,7 @@
 
 def exchange_kernel(
     patches, cols, own, coef, mate_out, cross_out, arrived,
-    mate_sems, cross_send, cross_recv, share_send, share_recv, coef_send, coef_recv, local_sem,
+    mate_sems, cross_send, cross_recv, up_send, down_send, share_recv, coef_send, coef_recv, local_sem,
 ):
     p = lax.axis_index("patch")
     c = lax.axis_index("col")
@@ -262,19 +262,16 @@
         at = c * per + k
         return remote(own.at[at], cross_out.at[at], cross_send.at[k], cross_recv.at[k], "patch", cross)
 
-    def share(j, k):
-        at = c * per + k
+    def pass_on(up, source, k):
+        at = source * per + k
+        send = up_send if up else down_send
+        peer = c + 1 if up else c - 1
         return remote(
-            cross_out.at[at], cross_out.at[at], share_send.at[j - 1, k], share_recv.at[j - 1, k],
-            "col", (c + j) % cols,
+            cross_out.at[at], cross_out.at[at], send.at[source, k], share_recv.at[source, k], "col", peer
         )
 
-    def shared(j, k):
-        at = ((c + cols - j) % cols) * per + k
-        return remote(
-            cross_out.at[at], cross_out.at[at], share_send.at[j - 1, k], share_recv.at[j - 1, k],
-            "col", (c + j) % cols,
-        )
+    not_first = c > 0
+    not_last = c < cols - 1
 
     def coefficients(j):
         q = (p + j) % patches
@@ -290,35 +287,73 @@
             coef_send.at[j - 1], coef_recv.at[j - 1], "patch", (p + j) % patches,
         )
 
+    to_mate = remote(own, mate_out, mate_sems.at[0], mate_sems.at[1], "patch", mate)
+    kept = pl.ds(p * capacity, capacity)
+    keep = pltpu.make_async_copy(coef.at[kept], arrived.at[kept], local_sem)
+
     @pl.when(crosses)
     def _():
         for k in range(per):
             crossing(k).start()
 
-    for j in range(1, patches):
-        coefficients(j).start()
-    to_mate = remote(own, mate_out, mate_sems.at[0], mate_sems.at[1], "patch", mate)
     to_mate.start()
-    kept = pl.ds(p * capacity, capacity)
-    keep = pltpu.make_async_copy(coef.at[kept], arrived.at[kept], local_sem)
     keep.start()
 
     @pl.when(crosses)
     def _():
         for k in range(per):
             crossing(k).wait_recv()
-            for j in range(1, cols):
-                share(j, k).start()
-        for k in range(per):
-            for j in range(1, cols):
-                shared(j, k).wait_recv()
+
+            @pl.when(not_last)
+            def _():
+                pass_on(True, c, k).start()
+
+            @pl.when(not_first)
+            def _():
+                pass_on(False, c, k).start()
+
+
+    to_mate.wait_recv()
+    for j in range(1, patches):
+        coefficients(j).start()
+
+    @pl.when(crosses)
+    def _():
+        for j in range(1, cols):
+            for k in range(per):
+                below, above = c - j, c + j
+
+                @pl.when(below >= 0)
+                def _():
+                    pass_on(True, below, k).wait_recv()
+
+                    @pl.when(not_last)
+                    def _():
+                        pass_on(True, below, k).start()
+
+                @pl.when(above < cols)
+                def _():
+                    pass_on(False, above, k).wait_recv()
+
+                    @pl.when(not_first)
+                    def _():
+                        pass_on(False, above, k).start()
+
         for k in range(per):
             crossing(k).wait_send()
-            for j in range(1, cols):
-                share(j, k).wait_send()
+            for j in range(cols):
+                below, above = c - j, c + j
+
+                @pl.when(jnp.logical_and(below >= 0, not_last))
+                def _():
+                    pass_on(True, below, k).wait_send()
+
+                @pl.when(jnp.logical_and(above < cols, not_first))
+                def _():
+                    pass_on(False, above, k).wait_send()
 
     keep.wait()
-    to_mate.wait()
+    to_mate.wait_send()
     for j in range(1, patches):
         coefficients_in(j).wait_recv()
         coefficients(j).wait_send()
@@ -340,8 +375,9 @@
             dma((2,)),
             dma((per,)),
             dma((per,)),
-            dma((cols - 1, per)),
-            dma((cols - 1, per)),
+            dma((cols, per)),
+            dma((cols, per)),
+            dma((cols, per)),
             dma((patches - 1,)),
             dma((patches - 1,)),
             dma(()),

time: 124 us -> 125 us (level)
    pallas_call x1, Pallas kernels: 45.5 us -> 55.2 us  [line_step(): pl.pallas_call(functools.partial(line_kernel, cols), in_specs=[pl.BlockSp...]
    pallas_call x1, Pallas kernels: 44 us -> 35.2 us  [exchange_step(): pl.pallas_call(functools.partial(exchange_kernel, patches, cols), in_spec...]
where the time goes in v4:
time: 125 us
  Pallas kernels  117 us (94%)
  local copies, waits for them, and re-layouts  6.85 us (5%)
    pallas_call x1, Pallas kernels, line_step(): pl.pallas_call(functools.partial(line_kernel, cols), in_specs=[pl.BlockSp...  55.2 us
    pallas_call x1, Pallas kernels, exchange_step(): pl.pallas_call(functools.partial(exchange_kernel, patches, cols), in_spec...  35.2 us
    pallas_call x1, Pallas kernels, target_step(): pl.pallas_call(functools.partial(target_kernel, near_count, rank_width),...  19.4 us
    unnamed x16, local copies, waits for them, and re-layouts  5.74 us
    pallas_call x1, Pallas kernels, call(): pl.pallas_call(functools.partial(source_kernel, far_count, rank_width), g...  5.33 us

profile of v4, /device:TPU:10, one launch (start us, length us, event | category | flops | bytes accessed | tf_op | source)
XLA Modules:
  0.0 125.1 jit_solution(12630207536633907998)
XLA Ops:
  0.0 0.7 fusion.1
  0.7 0.8 reshape.26.target_ref
  1.5 0.1 copy.15
  1.5 0.1 reshape.25.src_ref
  1.6 0.8 copy.16
  2.4 0.1 reshape.27.dest_ref
  2.5 0.8 copy.17
  3.2 0.1 reshape.28.rank_ref
  3.3 0.0 copy-start
  3.3 2.8 %copy-done = f32[256,3,2048]{2,0,1:T(8,128)S(1)} copy-done((f32[256,3,2048]{2,0,1:T(8,128)S(1)}, f32[256,3,2048]{2,0,1:T(8,128)}, u32[]{:S(2)}) %copy-start) | copy-done | bytes 6291480
  6.1 0.0 copy-start.2
  6.1 1.4 %copy-done.2 = bf16[1,16,4,32,384]{4,3,2,1,0:T(8,128)(2,1)S(1)} copy-done((bf16[1,16,4,32,384]{4,3,2,1,0:T(8,128)(2,1)S(1)}, bf16[1,16,4,32,384]{4,3,2,1,0:T(8,128)(2,1)}, u32[]{:S(2)}) %copy-start.2) | copy-done | bytes 1572888
  7.5 5.3 %source.1 = (bf16[16,256,384]{2,1,0:T(8,128)(2,1)S(1)}, bf16[128,32,256]{2,1,0:T(8,128)(2,1)S(1)}) custom-call(s32[64]{0:T(128)S(1)} %reshape.27.dest_ref, s32[64]{0:T(128)S(1)} %reshape.28.rank_ref, f32[3,4,1,64,2048]{4,3,2,1,0:T(8,128)S(1)} %bitcast.10, bf16[16,128,384]{2,1,0:T(8,128)(2,1)S(1)} %bitcast.16), custom_call_target="tpu_custom_call" | custom-call | flops 402653184 | bytes 8388608 | tf_op jit(solution)/shard_map/source/pallas_call | solution.py:46
  12.9 0.0 copy-start.1
  12.9 35.2 %exchange.1 = (bf16[16,256,384]{2,1,0:T(8,128)(2,1)S(1)}, bf16[16,256,384]{2,1,0:T(8,128)(2,1)S(1)}, bf16[128,32,256]{2,1,0:T(8,128)(2,1)S(1)}) custom-call(bf16[16,256,384]{2,1,0:T(8,128)(2,1)S(1)} %get-tuple-element.10.own.own_ref, bf16[128,32,256]{2,1,0:T(8,128)(2,1)S(1)} %get-tuple-element.11.coef), custom_call_target="tpu_custom_call" | custom-call | tf_op jit(solution)/shard_map/exchange/pallas_call | solution.py:365
  48.1 0.0 slice-start
  48.1 0.0 copy-done.1
  48.2 0.0 slice-start.1
  48.2 19.4 %target.1.part_ref = bf16[4,3,64,2048]{3,2,1,0:T(8,128)(2,1)S(1)} custom-call(s32[32]{0:T(128)S(1)} %reshape.25.src_ref, s32[128]{0:T(128)S(1)} %reshape.26.target_ref, bf16[16,256,384]{2,1,0:T(8,128)(2,1)S(1)} %get-tuple-element.12.mate_ref, bf16[16,256,384]{2,1,0:T(8,128)(2,1)S(1)} %get-tuple-element.10.own.own_ref, ...), custom_call_target="tpu_custom_call" | custom-call | flops 3221225472 | bytes 25165824 | tf_op jit(solution)/shard_map/target/pallas_call | solution.py:151
  67.6 0.0 copy-start.3
  67.6 0.0 copy-start.4
  67.6 55.2 %line.1 = f32[3,64,2048]{2,1,0:T(8,128)S(1)} custom-call(bf16[4,3,64,2048]{3,2,1,0:T(8,128)(2,1)S(1)} %target.1.part_ref), custom_call_target="tpu_custom_call" | custom-call | tf_op jit(solution)/shard_map/line/pallas_call | solution.py:504
  122.8 0.0 slice-done
  122.8 0.0 slice-done.1
  122.8 0.0 copy-done.3
  122.9 0.0 copy-done.4
  122.9 2.2 %law.1 = f32[3,64,2048]{2,1,0:T(8,128)} custom-call(s32[1]{0:T(128)} %bitcast.col_ref, f32[1,3,64,2048]{3,2,1,0:T(8,128)S(1)} %bitcast.14, f32[3,256,2048]{2,1,0:T(8,128)S(1)} %bitcast.13, f32[64,2048]{1,0:T(8,128)S(1)} %copy-done.3, f32[3,2048]{1,0:T(4,128)S(1)} %copy-done.4), custom_call_target="tpu_custom_call" | custom-call | flops 16777216 | bytes 8388608 | tf_op jit(solution)/shard_map/law/pallas_call | solution.py:210
  (1 shorter events, 0.0 us)
Async XLA Ops:
  3.3 2.8 %copy-start = (f32[256,3,2048]{2,0,1:T(8,128)S(1)}, f32[256,3,2048]{2,0,1:T(8,128)}, u32[]{:S(2)}) copy-start(f32[256,3,2048]{2,0,1:T(8,128)} %param.10) | copy-start | bytes 18874372
  6.1 1.4 %copy-start.2 = (bf16[1,16,4,32,384]{4,3,2,1,0:T(8,128)(2,1)S(1)}, bf16[1,16,4,32,384]{4,3,2,1,0:T(8,128)(2,1)}, u32[]{:S(2)}) copy-start(bf16[1,16,4,32,384]{4,3,2,1,0:T(8,128)(2,1)} %param.17) | copy-start | bytes 4718596
  12.9 35.3 %copy-start.1 = (bf16[1,1,4,32,32,384]{5,4,3,2,1,0:T(8,128)(2,1)S(1)}, bf16[1,1,4,32,32,384]{5,4,3,2,1,0:T(8,128)(2,1)}, u32[]{:S(2)}) copy-start(bf16[1,1,4,32,32,384]{5,4,3,2,1,0:T(8,128)(2,1)} %param.19) | copy-start | bytes 9437188
  48.1 74.7 %slice-start = ((s8[6291456]{0:T(1024)(128)(4,1)}), s8[4194304]{0:T(1024)(128)(4,1)S(1)}, s32[]{:S(2)}) async-start(s8[6291456]{0:T(1024)(128)(4,1)} %bitcast.11), calls=%async_computation | async-start | bytes 8388608
  48.2 74.7 %slice-start.1 = ((s8[6291456]{0:T(1024)(128)(4,1)}), s8[2097152]{0:T(1024)(128)(4,1)S(1)}, s32[]{:S(2)}) async-start(s8[6291456]{0:T(1024)(128)(4,1)} %bitcast.11), calls=%async_computation.1 | async-start | bytes 4194304
  67.6 55.3 %copy-start.3 = (f32[64,2048]{1,0:T(8,128)S(1)}, f32[64,2048]{1,0:T(8,128)}, u32[]{:S(2)}) copy-start(f32[64,2048]{1,0:T(8,128)} %refs_2_.1) | copy-start | bytes 1572868
  67.6 55.3 %copy-start.4 = (f32[3,2048]{1,0:T(4,128)S(1)}, f32[3,2048]{1,0:T(4,128)}, u32[]{:S(2)}) copy-start(f32[3,2048]{1,0:T(4,128)} %refs_3_.1) | copy-start | bytes 73732

commit v5 on v4

--- a/solution.py
+++ b/solution.py
@@ -8,7 +8,7 @@
 
 CS = 128
 CHUNKS = 1
-PIECES = 8
+PIECES = 4
 GROUP = 8
 MIB = 1 << 20
 MESH = pl.DeviceIdType.MESH

time: 125 us -> 125 us (level); the launches traced: 125 us -> 124 us
    pallas_call x1, Pallas kernels: 55.2 us -> 53.6 us  [line_step(): pl.pallas_call(functools.partial(line_kernel, cols), in_specs=[pl.BlockSp...]
where the time goes in v5:
time: 125 us; the launch traced here: 124 us
  Pallas kernels  116 us (93%)
  local copies, waits for them, and re-layouts  6.85 us (5%)
    pallas_call x1, Pallas kernels, line_step(): pl.pallas_call(functools.partial(line_kernel, cols), in_specs=[pl.BlockSp...  53.6 us
    pallas_call x1, Pallas kernels, exchange_step(): pl.pallas_call(functools.partial(exchange_kernel, patches, cols), in_spec...  35.2 us
    pallas_call x1, Pallas kernels, target_step(): pl.pallas_call(functools.partial(target_kernel, near_count, rank_width),...  19.6 us
    unnamed x16, local copies, waits for them, and re-layouts  5.74 us
    pallas_call x1, Pallas kernels, call(): pl.pallas_call(functools.partial(source_kernel, far_count, rank_width), g...  5.33 us

profile of v5, /device:TPU:10, one launch (start us, length us, event | category | flops | bytes accessed | tf_op | source)
XLA Modules:
  0.0 123.7 jit_solution(16132974457730714046)
XLA Ops:
  0.0 0.7 fusion.1
  0.7 0.8 reshape.26.target_ref
  1.5 0.1 copy.15
  1.5 0.1 reshape.25.src_ref
  1.6 0.8 copy.16
  2.4 0.1 reshape.27.dest_ref
  2.5 0.8 copy.17
  3.2 0.1 reshape.28.rank_ref
  3.3 0.0 copy-start
  3.3 2.8 %copy-done = f32[256,3,2048]{2,0,1:T(8,128)S(1)} copy-done((f32[256,3,2048]{2,0,1:T(8,128)S(1)}, f32[256,3,2048]{2,0,1:T(8,128)}, u32[]{:S(2)}) %copy-start) | copy-done | bytes 6291480
  6.1 0.0 copy-start.2
  6.1 1.4 %copy-done.2 = bf16[1,16,4,32,384]{4,3,2,1,0:T(8,128)(2,1)S(1)} copy-done((bf16[1,16,4,32,384]{4,3,2,1,0:T(8,128)(2,1)S(1)}, bf16[1,16,4,32,384]{4,3,2,1,0:T(8,128)(2,1)}, u32[]{:S(2)}) %copy-start.2) | copy-done | bytes 1572888
  7.5 5.3 %source.1 = (bf16[16,256,384]{2,1,0:T(8,128)(2,1)S(1)}, bf16[128,32,256]{2,1,0:T(8,128)(2,1)S(1)}) custom-call(s32[64]{0:T(128)S(1)} %reshape.27.dest_ref, s32[64]{0:T(128)S(1)} %reshape.28.rank_ref, f32[3,4,1,64,2048]{4,3,2,1,0:T(8,128)S(1)} %bitcast.10, bf16[16,128,384]{2,1,0:T(8,128)(2,1)S(1)} %bitcast.16), custom_call_target="tpu_custom_call" | custom-call | flops 402653184 | bytes 8388608 | tf_op jit(solution)/shard_map/source/pallas_call | solution.py:46
  12.9 0.0 copy-start.1
  12.9 35.2 %exchange.1 = (bf16[16,256,384]{2,1,0:T(8,128)(2,1)S(1)}, bf16[16,256,384]{2,1,0:T(8,128)(2,1)S(1)}, bf16[128,32,256]{2,1,0:T(8,128)(2,1)S(1)}) custom-call(bf16[16,256,384]{2,1,0:T(8,128)(2,1)S(1)} %get-tuple-element.10.own.own_ref, bf16[128,32,256]{2,1,0:T(8,128)(2,1)S(1)} %get-tuple-element.11.coef), custom_call_target="tpu_custom_call" | custom-call | tf_op jit(solution)/shard_map/exchange/pallas_call | solution.py:365
  48.1 0.0 slice-start
  48.1 0.0 copy-done.1
  48.2 0.0 slice-start.1
  48.2 19.6 %target.1.part_ref = bf16[4,3,64,2048]{3,2,1,0:T(8,128)(2,1)S(1)} custom-call(s32[32]{0:T(128)S(1)} %reshape.25.src_ref, s32[128]{0:T(128)S(1)} %reshape.26.target_ref, bf16[16,256,384]{2,1,0:T(8,128)(2,1)S(1)} %get-tuple-element.12.mate_ref, bf16[16,256,384]{2,1,0:T(8,128)(2,1)S(1)} %get-tuple-element.10.own.own_ref, ...), custom_call_target="tpu_custom_call" | custom-call | flops 3221225472 | bytes 25165824 | tf_op jit(solution)/shard_map/target/pallas_call | solution.py:151
  67.7 0.0 copy-start.3
  67.8 0.0 copy-start.4
  67.8 53.6 %line.1 = f32[3,64,2048]{2,1,0:T(8,128)S(1)} custom-call(bf16[4,3,64,2048]{3,2,1,0:T(8,128)(2,1)S(1)} %target.1.part_ref), custom_call_target="tpu_custom_call" | custom-call | tf_op jit(solution)/shard_map/line/pallas_call | solution.py:504
  121.4 0.0 slice-done
  121.4 0.0 slice-done.1
  121.4 0.0 copy-done.3
  121.4 0.0 copy-done.4
  121.4 2.2 %law.1 = f32[3,64,2048]{2,1,0:T(8,128)} custom-call(s32[1]{0:T(128)} %bitcast.col_ref, f32[1,3,64,2048]{3,2,1,0:T(8,128)S(1)} %bitcast.14, f32[3,256,2048]{2,1,0:T(8,128)S(1)} %bitcast.13, f32[64,2048]{1,0:T(8,128)S(1)} %copy-done.3, f32[3,2048]{1,0:T(4,128)S(1)} %copy-done.4), custom_call_target="tpu_custom_call" | custom-call | flops 16777216 | bytes 8388608 | tf_op jit(solution)/shard_map/law/pallas_call | solution.py:210
  (1 shorter events, 0.0 us)
Async XLA Ops:
  3.3 2.8 %copy-start = (f32[256,3,2048]{2,0,1:T(8,128)S(1)}, f32[256,3,2048]{2,0,1:T(8,128)}, u32[]{:S(2)}) copy-start(f32[256,3,2048]{2,0,1:T(8,128)} %param.10) | copy-start | bytes 18874372
  6.1 1.4 %copy-start.2 = (bf16[1,16,4,32,384]{4,3,2,1,0:T(8,128)(2,1)S(1)}, bf16[1,16,4,32,384]{4,3,2,1,0:T(8,128)(2,1)}, u32[]{:S(2)}) copy-start(bf16[1,16,4,32,384]{4,3,2,1,0:T(8,128)(2,1)} %param.17) | copy-start | bytes 4718596
  12.9 35.3 %copy-start.1 = (bf16[1,1,4,32,32,384]{5,4,3,2,1,0:T(8,128)(2,1)S(1)}, bf16[1,1,4,32,32,384]{5,4,3,2,1,0:T(8,128)(2,1)}, u32[]{:S(2)}) copy-start(bf16[1,1,4,32,32,384]{5,4,3,2,1,0:T(8,128)(2,1)} %param.19) | copy-start | bytes 9437188
  48.1 73.2 %slice-start = ((s8[6291456]{0:T(1024)(128)(4,1)}), s8[4194304]{0:T(1024)(128)(4,1)S(1)}, s32[]{:S(2)}) async-start(s8[6291456]{0:T(1024)(128)(4,1)} %bitcast.11), calls=%async_computation | async-start | bytes 8388608
  48.2 73.2 %slice-start.1 = ((s8[6291456]{0:T(1024)(128)(4,1)}), s8[2097152]{0:T(1024)(128)(4,1)S(1)}, s32[]{:S(2)}) async-start(s8[6291456]{0:T(1024)(128)(4,1)} %bitcast.11), calls=%async_computation.1 | async-start | bytes 4194304
  67.7 53.6 %copy-start.3 = (f32[64,2048]{1,0:T(8,128)S(1)}, f32[64,2048]{1,0:T(8,128)}, u32[]{:S(2)}) copy-start(f32[64,2048]{1,0:T(8,128)} %refs_2_.1) | copy-start | bytes 1572868
  67.8 53.6 %copy-start.4 = (f32[3,2048]{1,0:T(4,128)S(1)}, f32[3,2048]{1,0:T(4,128)}, u32[]{:S(2)}) copy-start(f32[3,2048]{1,0:T(4,128)} %refs_3_.1) | copy-start | bytes 73732
